TPU v7x, 1024 devices: a whole 8x8x8 slice. The times are simulated.
1024 devices in a mesh: face: 16 (over x, core), tile: 64 (over z, y).
Axes of the slice: x: 8, y: 8, z: 8, core: 2. Of those that a mesh axis runs over, the one named last changes fastest.
Arguments:
- ocean_forcing: bfloat16 [16, 8192, 4, 128], P('face', 'tile'), may hold values from -5 to 5
- ice_owner: int32 [16, 8192], P('face', 'tile'), may hold values from 0 to 15, as said below
- ice_mask: int32 [16, 8192], P('face', 'tile'), may hold values 0 or 1
- ice_velocity: float32 [2, 16, 512, 2048], P(None, 'face', 'tile'), may hold values from -4 to 4
- ice_mass: float32 [16, 512, 2048], P('face', 'tile'), may hold values from 0.35 to 0.7
- ice_strength: float32 [16, 512, 2048], P('face', 'tile'), may hold values from 1.5 to 3
Outputs:
- velocity_out: float32 [2, 16, 512, 2048], P(None, 'face', 'tile')
- ocean_drag: bfloat16 [16, 8192, 2, 128], P('face', 'tile')
Inputs may be any that keep to these rules, and one draw needn't show every extreme that they name: `ice_owner`: within each aligned block of 128 entries of a row (one ocean tile's blocks, aligned), every face index appears exactly 8 times.
All inputs are finite; a program needn't handle non-finite values. No bound on the sum of `ice_mask` on one device may be relied on, other than what follows from the above.
Results may differ from a plain program's by a relative error of at most 0.001.
Values may be sent and summed in bfloat16 or wider, within the bound.
A program may use at most 32 MiB of HBM per device.

v0:
```python
import jax
import jax.numpy as jnp
from jax import lax
from jax.sharding import PartitionSpec as P

ITERS = 8


ECC2 = 4.0
DMIN2 = 0.01
CE = 0.5
DTS = 0.25
CW = 1.0
COR = 0.5


def extended(cells, sides, width):
    for axis, dim in sides:
        count = lax.axis_size(axis)
        head = lax.slice_in_dim(cells, 0, width, axis=dim)
        tail = lax.slice_in_dim(cells, cells.shape[dim] - width, cells.shape[dim], axis=dim)
        cells = jnp.concatenate(
            [
                lax.ppermute(tail, axis, [(i, (i + 1) % count) for i in range(count)]),
                cells,
                lax.ppermute(head, axis, [((i + 1) % count, i) for i in range(count)]),
            ],
            axis=dim,
        )
    return cells


def edge_fix(padded, signs):
    face = lax.axis_index("face")
    tile = lax.axis_index("tile")
    faces = lax.axis_size("face")
    tiles = lax.axis_size("tile")
    lower = padded[:, 0]
    upper = padded[:, -1]
    lower_flip = (tile == 0) & ((face + faces - 1) % 2 == 1)
    upper_flip = (tile == tiles - 1) & (face % 2 == 1)
    lower = jnp.where(lower_flip, signs[:, None] * lower[:, ::-1], lower)
    upper = jnp.where(upper_flip, signs[:, None] * upper[:, ::-1], upper)
    return jnp.concatenate([lower[:, None], padded[:, 1:-1], upper[:, None]], axis=1)


def slope_x(inner):
    return 0.5 * (jnp.roll(inner, -1, -1) - jnp.roll(inner, 1, -1))


def slope_y(padded):
    return 0.5 * (padded[..., 2:, :] - padded[..., :-2, :])


def stress_update(padded_vel, stress, strength, cover):
    e11 = slope_x(padded_vel[0][..., 1:-1, :])
    e22 = slope_y(padded_vel[1])
    e12 = 0.5 * (slope_y(padded_vel[0]) + slope_x(padded_vel[1][..., 1:-1, :]))
    dd = e11 + e22
    dtn = e11 - e22
    dsh = 2.0 * e12
    delta = jnp.sqrt(dd * dd + (dtn * dtn + dsh * dsh) / ECC2 + DMIN2)
    first = cover * (stress[0] + CE * strength * (dd / delta - 1.0)) / (1.0 + CE)
    second = cover * (stress[1] + CE * strength * dtn / (ECC2 * delta)) / (1.0 + CE)
    shear = cover * (stress[2] + CE * strength * dsh / (2.0 * ECC2 * delta)) / (1.0 + CE)
    return jnp.stack([first, second, shear])


def momentum_update(velocity, padded_stress, mass, forcing, cover):
    s11 = 0.5 * (padded_stress[0] + padded_stress[1])
    s22 = 0.5 * (padded_stress[0] - padded_stress[1])
    s12 = padded_stress[2]
    force_x = slope_x(s11[..., 1:-1, :]) + slope_y(s12)
    force_y = slope_x(s12[..., 1:-1, :]) + slope_y(s22)
    east, north = (velocity[0], velocity[1])
    diff_u = forcing[0] - east
    diff_v = forcing[1] - north
    speed = jnp.sqrt(diff_u * diff_u + diff_v * diff_v)
    damping = 1.0 + DTS * CW * speed / mass
    new_u = (
        cover
        * (
            east
            + DTS / mass * (force_x + forcing[2] + CW * speed * forcing[0] + COR * mass * north)
        )
        / damping
    )
    new_v = (
        cover
        * (
            north
            + DTS / mass * (force_y + forcing[3] + CW * speed * forcing[1] - COR * mass * east)
        )
        / damping
    )
    return jnp.stack([new_u, new_v])


def per_device(ocean_forcing, ice_owner, ice_mask, ice_velocity, ice_mass, ice_strength):
    faces = lax.axis_size("face")
    own_face = lax.axis_index("face")
    owner = ice_owner[0]
    blocks_dev = owner.shape[0]
    pair = blocks_dev // faces
    rows = ice_mass.shape[1]
    width = ice_mass.shape[2]
    cols = width // 128
    onehot = (owner[:, None] == jnp.arange(faces, dtype=jnp.int32)[None, :]).astype(jnp.int32)
    rank = jnp.sum(jnp.cumsum(onehot, axis=0) * onehot, axis=1) - 1
    position = owner * pair + rank
    sorter = (jnp.arange(blocks_dev, dtype=jnp.int32)[:, None] == position[None, :]).astype(
        jnp.bfloat16
    )
    blocks = ocean_forcing.reshape(blocks_dev, 512)
    grouped = jnp.dot(sorter, blocks, preferred_element_type=jnp.float32).astype(jnp.bfloat16)
    grouped = grouped.reshape(faces, pair, 512)

    def take_mine(piece):
        mine = lax.dynamic_index_in_dim(piece, own_face, 1, keepdims=False)
        return mine

    arrived = take_mine(lax.all_gather(grouped[None], "face", axis=0, tiled=True))
    forcing = (
        arrived.reshape(rows, cols, 4, 128)
        .transpose(2, 0, 1, 3)
        .reshape(4, rows, width)
        .astype(jnp.float32)
    )
    cover = jnp.broadcast_to(
        ice_mask[0].reshape(rows, cols, 1).astype(jnp.float32), (rows, cols, 128)
    ).reshape(rows, width)
    mass = ice_mass[0]
    strength = ice_strength[0]
    vel_signs = jnp.array([-1.0, 1.0], jnp.float32)
    stress_signs = jnp.array([1.0, 1.0, -1.0], jnp.float32)
    velocity = ice_velocity[:, 0]
    stress = jnp.zeros((3, rows, width), jnp.float32)
    for step in range(ITERS):
        padded_vel = extended(velocity, ((("face", "tile"), 1),), 1)
        stress = stress_update(edge_fix(padded_vel, vel_signs), stress, strength, cover)
        padded_stress = extended(stress, ((("face", "tile"), 1),), 1)
        velocity = momentum_update(
            velocity, edge_fix(padded_stress, stress_signs), mass, forcing, cover
        )
    diff_u = forcing[0] - velocity[0]
    diff_v = forcing[1] - velocity[1]
    speed = jnp.sqrt(diff_u * diff_u + diff_v * diff_v)
    drag = jnp.stack([cover * CW * speed * -diff_u, cover * CW * speed * -diff_v]).astype(
        jnp.bfloat16
    )
    drag_blocks = drag.reshape(2, rows, cols, 128).transpose(1, 2, 0, 3).reshape(faces, pair, 256)
    returned = take_mine(lax.all_gather(drag_blocks[None], "face", axis=0, tiled=True))
    returned = returned.reshape(blocks_dev, 256)
    ocean_drag = jnp.dot(sorter.T, returned, preferred_element_type=jnp.float32).astype(
        jnp.bfloat16
    )
    return (velocity[:, None], ocean_drag.reshape(1, blocks_dev, 2, 128))


def solution(mesh):
    in_specs = (
        P("face", "tile", None, None),
        P("face", "tile"),
        P("face", "tile"),
        P(None, "face", "tile", None),
        P("face", "tile", None),
        P("face", "tile", None),
    )
    out_specs = (P(None, "face", "tile", None), P("face", "tile", None, None))
    return jax.shard_map(
        per_device, mesh=mesh, in_specs=in_specs, out_specs=out_specs, check_vma=False
    )
```

profile of v0, /device:TPU:1, one launch (start us, length us, event | category | flops | bytes accessed | tf_op | source)
XLA Modules:
  0.0 346.5 jit_solution(8987251888452148550)
XLA Ops:
  9.6 1.7 fusion
  12.5 22.1 %collective-permute-start = (f32[2,1,2048]{2,0,1:T(2,128)S(1)}, f32[2,1,2048]{2,0,1:T(2,128)S(1)}, u32[]{:S(2)}, u32[]{:S(2)}) collective-permute-start(f32[2,1,2048]{2,0,1:T(2,128)S(1)} %get-tuple-element.133), channel_id=1, source_target_pairs={{1,0},{2,1},{3,2},{4,3},{5,4},{6,5},{7,6},{8,7},{9,8},{10,9},{11,1... | collective-permute-start | bytes 49160 | tf_op jit(solution)/shard_map/ppermute | solution.py:26
  34.6 1.9 collective-permute-start.1
  38.6 1.4 rev.96
  40.0 3.0 collective-permute-done.1
  43.0 1.4 rev.97
  45.1 1.9 collective-permute-start.2
  47.0 7.0 %collective-permute-start.3 = (f32[3,1,2048]{2,0,1:T(4,128)S(1)}, f32[3,1,2048]{2,0,1:T(4,128)S(1)}, u32[]{:S(2)}, u32[]{:S(2)}) collective-permute-start(f32[3,1,2048]{2,0,1:T(4,128)S(1)} %copy.495), channel_id=1, source_target_pairs={{1,0},{2,1},{3,2},{4,3},{5,4},{6,5},{7,6},{8,7},{9,8},{10,9},{11,1... | collective-permute-start | bytes 73736 | tf_op jit(solution)/shard_map/ppermute | solution.py:26
  54.2 1.4 rev.98
  55.6 1.4 rev.99
  57.4 11.4 %all-gather.3.cloned.1.call-done = bf16[16,16,8,512]{3,2,1,0:T(8,128)(2,1)} async-done(((bf16[1,16,8,512]{3,2,1,0:T(8,128)(2,1)}), bf16[16,16,8,512]{3,2,1,0:T(8,128)(2,1)}) %all-gather.3.cloned.1.call-update) | async-done | bytes 2097168 | tf_op jit(solution)/shard_map/all_gather | solution.py:122
  70.5 9.1 %collective-permute-start.4 = (f32[2,1,2048]{2,0,1:T(2,128)S(1)}, f32[2,1,2048]{2,0,1:T(2,128)S(1)}, u32[]{:S(2)}, u32[]{:S(2)}) collective-permute-start(f32[2,1,2048]{2,0,1:T(2,128)S(1)} %copy.496), channel_id=1, source_target_pairs={{1,0},{2,1},{3,2},{4,3},{5,4},{6,5},{7,6},{8,7},{9,8},{10,9},{11,1... | collective-permute-start | bytes 49160 | tf_op jit(solution)/shard_map/ppermute | solution.py:26
  79.6 1.9 collective-permute-start.5
  81.6 1.4 rev.100
  83.0 5.0 %collective-permute-done.5 = f32[2,1,2048]{2,0,1:T(2,128)S(1)} collective-permute-done((f32[2,1,2048]{2,0,1:T(2,128)S(1)}, f32[2,1,2048]{2,0,1:T(2,128)S(1)}, u32[]{:S(2)}, u32[]{:S(2)}) %collective-permute-start.5) | collective-permute-done | bytes 16416 | tf_op jit(solution)/shard_map/ppermute | solution.py:24
  88.0 1.4 rev.101
  89.8 2.0 collective-permute-start.7
  91.8 3.3 collective-permute-start.6
  96.7 3.7 %collective-permute-done.6 = f32[3,1,2048]{2,0,1:T(4,128)S(1)} collective-permute-done((f32[3,1,2048]{2,0,1:T(4,128)S(1)}, f32[3,1,2048]{2,0,1:T(4,128)S(1)}, u32[]{:S(2)}, u32[]{:S(2)}) %collective-permute-start.6) | collective-permute-done | bytes 24608 | tf_op jit(solution)/shard_map/ppermute | solution.py:24
  100.4 1.4 rev.102
  103.2 1.9 collective-permute-start.8
  105.2 3.4 collective-permute-start.9
  108.6 1.4 rev.104
  110.0 3.5 %collective-permute-done.9 = f32[2,1,2048]{2,0,1:T(2,128)S(1)} collective-permute-done((f32[2,1,2048]{2,0,1:T(2,128)S(1)}, f32[2,1,2048]{2,0,1:T(2,128)S(1)}, u32[]{:S(2)}, u32[]{:S(2)}) %collective-permute-start.9) | collective-permute-done | bytes 16416 | tf_op jit(solution)/shard_map/ppermute | solution.py:24
  113.5 1.4 rev.105
  115.7 2.0 collective-permute-start.11
  117.7 3.3 collective-permute-start.10
  121.2 1.4 rev.107
  122.6 3.7 %collective-permute-done.10 = f32[3,1,2048]{2,0,1:T(4,128)S(1)} collective-permute-done((f32[3,1,2048]{2,0,1:T(4,128)S(1)}, f32[3,1,2048]{2,0,1:T(4,128)S(1)}, u32[]{:S(2)}, u32[]{:S(2)}) %collective-permute-start.10) | collective-permute-done | bytes 24608 | tf_op jit(solution)/shard_map/ppermute | solution.py:24
  128.8 1.9 collective-permute-start.12
  130.7 3.4 collective-permute-start.13
  134.3 1.4 rev.108
  135.7 3.4 collective-permute-done.13
  141.9 1.9 collective-permute-start.14
  143.9 7.0 %collective-permute-start.15 = (f32[3,1,2048]{2,0,1:T(4,128)S(1)}, f32[3,1,2048]{2,0,1:T(4,128)S(1)}, u32[]{:S(2)}, u32[]{:S(2)}) collective-permute-start(f32[3,1,2048]{2,0,1:T(4,128)S(1)} %get-tuple-element.54), channel_id=1, source_target_pairs={{1,0},{2,1},{3,2},{4,3},{5,4},{6,5},{7,6},{8,7},{9,8},{10,9},{11,1... | collective-permute-start | bytes 73736 | tf_op jit(solution)/shard_map/ppermute | solution.py:26
  151.1 1.4 rev.110
  155.2 6.8 %collective-permute-start.16 = (f32[2,1,2048]{2,0,1:T(2,128)S(1)}, f32[2,1,2048]{2,0,1:T(2,128)S(1)}, u32[]{:S(2)}, u32[]{:S(2)}) collective-permute-start(f32[2,1,2048]{2,0,1:T(2,128)S(1)} %get-tuple-element.101), channel_id=1, source_target_pairs={{1,0},{2,1},{3,2},{4,3},{5,4},{6,5},{7,6},{8,7},{9,8},{10,9},{11,1... | collective-permute-start | bytes 49160 | tf_op jit(solution)/shard_map/ppermute | solution.py:26
  162.0 1.9 collective-permute-start.17
  164.2 1.4 rev.112
  165.6 4.7 %collective-permute-done.17 = f32[2,1,2048]{2,0,1:T(2,128)S(1)} collective-permute-done((f32[2,1,2048]{2,0,1:T(2,128)S(1)}, f32[2,1,2048]{2,0,1:T(2,128)S(1)}, u32[]{:S(2)}, u32[]{:S(2)}) %collective-permute-start.17) | collective-permute-done | bytes 16416 | tf_op jit(solution)/shard_map/ppermute | solution.py:24
  172.9 2.2 collective-permute-start.19
  175.2 3.1 collective-permute-start.18
  179.8 3.9 %collective-permute-done.18 = f32[3,1,2048]{2,0,1:T(4,128)S(1)} collective-permute-done((f32[3,1,2048]{2,0,1:T(4,128)S(1)}, f32[3,1,2048]{2,0,1:T(4,128)S(1)}, u32[]{:S(2)}, u32[]{:S(2)}) %collective-permute-start.18) | collective-permute-done | bytes 24608 | tf_op jit(solution)/shard_map/ppermute | solution.py:24
  186.2 1.9 collective-permute-start.20
  188.2 3.5 %collective-permute-start.21 = (f32[2,1,2048]{2,0,1:T(2,128)S(1)}, f32[2,1,2048]{2,0,1:T(2,128)S(1)}, u32[]{:S(2)}, u32[]{:S(2)}) collective-permute-start(f32[2,1,2048]{2,0,1:T(2,128)S(1)} %get-tuple-element.96), channel_id=1, source_target_pairs={{0,1},{1,2},{2,3},{3,4},{4,5},{5,6},{6,7},{7,8},{8,9},{9,10},{10,1... | collective-permute-start | bytes 49160 | tf_op jit(solution)/shard_map/ppermute | solution.py:24
  192.0 1.4 rev.116
  193.4 3.1 collective-permute-done.21
  199.1 2.4 collective-permute-start.23
  201.5 2.9 collective-permute-start.22
  206.0 4.1 %collective-permute-done.22 = f32[3,1,2048]{2,0,1:T(4,128)S(1)} collective-permute-done((f32[3,1,2048]{2,0,1:T(4,128)S(1)}, f32[3,1,2048]{2,0,1:T(4,128)S(1)}, u32[]{:S(2)}, u32[]{:S(2)}) %collective-permute-start.22) | collective-permute-done | bytes 24608 | tf_op jit(solution)/shard_map/ppermute | solution.py:24
  212.8 1.9 collective-permute-start.24
  214.7 3.4 collective-permute-start.25
  219.5 3.5 %collective-permute-done.25 = f32[2,1,2048]{2,0,1:T(2,128)S(1)} collective-permute-done((f32[2,1,2048]{2,0,1:T(2,128)S(1)}, f32[2,1,2048]{2,0,1:T(2,128)S(1)}, u32[]{:S(2)}, u32[]{:S(2)}) %collective-permute-start.25) | collective-permute-done | bytes 16416 | tf_op jit(solution)/shard_map/ppermute | solution.py:24
  225.5 1.9 collective-permute-start.26
  227.4 7.0 %collective-permute-start.27 = (f32[3,1,2048]{2,0,1:T(4,128)S(1)}, f32[3,1,2048]{2,0,1:T(4,128)S(1)}, u32[]{:S(2)}, u32[]{:S(2)}) collective-permute-start(f32[3,1,2048]{2,0,1:T(4,128)S(1)} %get-tuple-element.52), channel_id=1, source_target_pairs={{1,0},{2,1},{3,2},{4,3},{5,4},{6,5},{7,6},{8,7},{9,8},{10,9},{11,1... | collective-permute-start | bytes 73736 | tf_op jit(solution)/shard_map/ppermute | solution.py:26
  234.7 1.4 rev.122
  238.7 6.8 %collective-permute-start.28 = (f32[2,1,2048]{2,0,1:T(2,128)S(1)}, f32[2,1,2048]{2,0,1:T(2,128)S(1)}, u32[]{:S(2)}, u32[]{:S(2)}) collective-permute-start(f32[2,1,2048]{2,0,1:T(2,128)S(1)} %get-tuple-element.81), channel_id=1, source_target_pairs={{1,0},{2,1},{3,2},{4,3},{5,4},{6,5},{7,6},{8,7},{9,8},{10,9},{11,1... | collective-permute-start | bytes 49160 | tf_op jit(solution)/shard_map/ppermute | solution.py:26
  245.6 1.9 collective-permute-start.29
  247.7 1.4 rev.124
  249.1 4.8 %collective-permute-done.29 = f32[2,1,2048]{2,0,1:T(2,128)S(1)} collective-permute-done((f32[2,1,2048]{2,0,1:T(2,128)S(1)}, f32[2,1,2048]{2,0,1:T(2,128)S(1)}, u32[]{:S(2)}, u32[]{:S(2)}) %collective-permute-start.29) | collective-permute-done | bytes 16416 | tf_op jit(solution)/shard_map/ppermute | solution.py:24
  256.1 2.1 collective-permute-start.31
  258.3 3.2 collective-permute-start.30
  263.0 3.8 %collective-permute-done.30 = f32[3,1,2048]{2,0,1:T(4,128)S(1)} collective-permute-done((f32[3,1,2048]{2,0,1:T(4,128)S(1)}, f32[3,1,2048]{2,0,1:T(4,128)S(1)}, u32[]{:S(2)}, u32[]{:S(2)}) %collective-permute-start.30) | collective-permute-done | bytes 24608 | tf_op jit(solution)/shard_map/ppermute | solution.py:24
  270.6 67.3 %all-gather.5.cloned.1.call-done = bf16[16,16,8,256]{3,2,1,0:T(8,128)(2,1)} async-done(((bf16[1,16,8,256]{3,2,1,0:T(8,128)(2,1)}), bf16[16,16,8,256]{3,2,1,0:T(8,128)(2,1)}) %all-gather.5.cloned.1.call-update) | async-done | bytes 1048592 | tf_op jit(solution)/shard_map/all_gather | solution.py:152
  (301 shorter events, 50.6 us)
Async XLA Ops:
  7.2 37.2 %copy-start.4 = (f32[2]{0:T(128)S(1)}, f32[2]{0:T(128)}, u32[]{:S(2)}) copy-start(f32[2]{0:T(128)} %constant.189.clone) | copy-start | bytes 28
  7.2 37.6 %copy-start.1 = (f32[1,8,2048]{2,1,0:T(8,128)S(1)}, f32[1,8,2048]{2,1,0:T(8,128)}, u32[]{:S(2)}) copy-start(f32[1,8,2048]{2,1,0:T(8,128)} %param.13) | copy-start | bytes 196612
  7.2 61.6 %all-gather.3.cloned.1.call-start = ((), (), s32[]{:S(2)}) async-start(), calls=%async_computation | async-start | bytes 2228224 | tf_op jit(solution)/shard_map/all_gather | solution.py:122
  11.4 45.6 %copy-start.3 = (f32[3]{0:T(128)S(1)}, f32[3]{0:T(128)}, u32[]{:S(2)}) copy-start(f32[3]{0:T(128)} %constant.190.clone) | copy-start | bytes 40
  11.4 326.5 %all-gather.5.cloned.1.call-start = ((), (), s32[]{:S(2)}) async-start(), calls=%async_computation.1 | async-start | bytes 1114112 | tf_op jit(solution)/shard_map/all_gather | solution.py:152
  12.5 26.1 %collective-permute-start = (f32[2,1,2048]{2,0,1:T(2,128)S(1)}, f32[2,1,2048]{2,0,1:T(2,128)S(1)}, u32[]{:S(2)}, u32[]{:S(2)}) collective-permute-start(f32[2,1,2048]{2,0,1:T(2,128)S(1)} %get-tuple-element.133), channel_id=1, source_target_pairs={{1,0},{2,1},{3,2},{4,3},{5,4},{6,5},{7,6},{8,7},{9,8},{10,9},{11,1... | collective-permute-start | bytes 49160 | tf_op jit(solution)/shard_map/ppermute | solution.py:26
  34.6 8.4 %collective-permute-start.1 = (f32[2,1,2048]{2,0,1:T(2,128)S(1)}, f32[2,1,2048]{2,0,1:T(2,128)S(1)}, u32[]{:S(2)}, u32[]{:S(2)}) collective-permute-start(f32[2,1,2048]{2,0,1:T(2,128)S(1)} %get-tuple-element.134), channel_id=1, source_target_pairs={{0,1},{1,2},{2,3},{3,4},{4,5},{5,6},{6,7},{7,8},{8,9},{9,10},{10,1... | collective-permute-start | bytes 49160 | tf_op jit(solution)/shard_map/ppermute | solution.py:24
  44.9 25.1 %copy-start = (f32[1,8,2048]{2,1,0:T(8,128)S(1)}, f32[1,8,2048]{2,1,0:T(8,128)}, u32[]{:S(2)}) copy-start(f32[1,8,2048]{2,1,0:T(8,128)} %param.12) | copy-start | bytes 196612
  44.9 25.1 %copy-start.2 = (f32[2,1,8,2048]{3,2,1,0:T(8,128)S(1)}, f32[2,1,8,2048]{3,2,1,0:T(8,128)}, u32[]{:S(2)}) copy-start(f32[2,1,8,2048]{3,2,1,0:T(8,128)} %param.11) | copy-start | bytes 393220
  45.1 9.1 %collective-permute-start.2 = (f32[3,1,2048]{2,0,1:T(4,128)S(1)}, f32[3,1,2048]{2,0,1:T(4,128)S(1)}, u32[]{:S(2)}, u32[]{:S(2)}) collective-permute-start(f32[3,1,2048]{2,0,1:T(4,128)S(1)} %copy.494), channel_id=1, source_target_pairs={{0,1},{1,2},{2,3},{3,4},{4,5},{5,6},{6,7},{7,8},{8,9},{9,10},{10,1... | collective-permute-start | bytes 73736 | tf_op jit(solution)/shard_map/ppermute | solution.py:24
  47.0 8.5 %collective-permute-start.3 = (f32[3,1,2048]{2,0,1:T(4,128)S(1)}, f32[3,1,2048]{2,0,1:T(4,128)S(1)}, u32[]{:S(2)}, u32[]{:S(2)}) collective-permute-start(f32[3,1,2048]{2,0,1:T(4,128)S(1)} %copy.495), channel_id=1, source_target_pairs={{1,0},{2,1},{3,2},{4,3},{5,4},{6,5},{7,6},{8,7},{9,8},{10,9},{11,1... | collective-permute-start | bytes 73736 | tf_op jit(solution)/shard_map/ppermute | solution.py:26
  70.5 11.1 %collective-permute-start.4 = (f32[2,1,2048]{2,0,1:T(2,128)S(1)}, f32[2,1,2048]{2,0,1:T(2,128)S(1)}, u32[]{:S(2)}, u32[]{:S(2)}) collective-permute-start(f32[2,1,2048]{2,0,1:T(2,128)S(1)} %copy.496), channel_id=1, source_target_pairs={{1,0},{2,1},{3,2},{4,3},{5,4},{6,5},{7,6},{8,7},{9,8},{10,9},{11,1... | collective-permute-start | bytes 49160 | tf_op jit(solution)/shard_map/ppermute | solution.py:26
  79.6 8.4 %collective-permute-start.5 = (f32[2,1,2048]{2,0,1:T(2,128)S(1)}, f32[2,1,2048]{2,0,1:T(2,128)S(1)}, u32[]{:S(2)}, u32[]{:S(2)}) collective-permute-start(f32[2,1,2048]{2,0,1:T(2,128)S(1)} %copy.497), channel_id=1, source_target_pairs={{0,1},{1,2},{2,3},{3,4},{4,5},{5,6},{6,7},{7,8},{8,9},{9,10},{10,1... | collective-permute-start | bytes 49160 | tf_op jit(solution)/shard_map/ppermute | solution.py:24
  89.8 5.5 %collective-permute-start.7 = (f32[3,1,2048]{2,0,1:T(4,128)S(1)}, f32[3,1,2048]{2,0,1:T(4,128)S(1)}, u32[]{:S(2)}, u32[]{:S(2)}) collective-permute-start(f32[3,1,2048]{2,0,1:T(4,128)S(1)} %copy.499), channel_id=1, source_target_pairs={{1,0},{2,1},{3,2},{4,3},{5,4},{6,5},{7,6},{8,7},{9,8},{10,9},{11,1... | collective-permute-start | bytes 73736 | tf_op jit(solution)/shard_map/ppermute | solution.py:26
  91.8 8.6 %collective-permute-start.6 = (f32[3,1,2048]{2,0,1:T(4,128)S(1)}, f32[3,1,2048]{2,0,1:T(4,128)S(1)}, u32[]{:S(2)}, u32[]{:S(2)}) collective-permute-start(f32[3,1,2048]{2,0,1:T(4,128)S(1)} %copy.498), channel_id=1, source_target_pairs={{0,1},{1,2},{2,3},{3,4},{4,5},{5,6},{6,7},{7,8},{8,9},{9,10},{10,1... | collective-permute-start | bytes 73736 | tf_op jit(solution)/shard_map/ppermute | solution.py:24
  103.2 5.4 %collective-permute-start.8 = (f32[2,1,2048]{2,0,1:T(2,128)S(1)}, f32[2,1,2048]{2,0,1:T(2,128)S(1)}, u32[]{:S(2)}, u32[]{:S(2)}) collective-permute-start(f32[2,1,2048]{2,0,1:T(2,128)S(1)} %get-tuple-element.113), channel_id=1, source_target_pairs={{1,0},{2,1},{3,2},{4,3},{5,4},{6,5},{7,6},{8,7},{9,8},{10,9},{11,1... | collective-permute-start | bytes 49160 | tf_op jit(solution)/shard_map/ppermute | solution.py:26
  105.2 8.4 %collective-permute-start.9 = (f32[2,1,2048]{2,0,1:T(2,128)S(1)}, f32[2,1,2048]{2,0,1:T(2,128)S(1)}, u32[]{:S(2)}, u32[]{:S(2)}) collective-permute-start(f32[2,1,2048]{2,0,1:T(2,128)S(1)} %get-tuple-element.114), channel_id=1, source_target_pairs={{0,1},{1,2},{2,3},{3,4},{4,5},{5,6},{6,7},{7,8},{8,9},{9,10},{10,1... | collective-permute-start | bytes 49160 | tf_op jit(solution)/shard_map/ppermute | solution.py:24
  115.7 5.5 %collective-permute-start.11 = (f32[3,1,2048]{2,0,1:T(4,128)S(1)}, f32[3,1,2048]{2,0,1:T(4,128)S(1)}, u32[]{:S(2)}, u32[]{:S(2)}) collective-permute-start(f32[3,1,2048]{2,0,1:T(4,128)S(1)} %copy.501), channel_id=1, source_target_pairs={{1,0},{2,1},{3,2},{4,3},{5,4},{6,5},{7,6},{8,7},{9,8},{10,9},{11,1... | collective-permute-start | bytes 73736 | tf_op jit(solution)/shard_map/ppermute | solution.py:26
  117.7 8.6 %collective-permute-start.10 = (f32[3,1,2048]{2,0,1:T(4,128)S(1)}, f32[3,1,2048]{2,0,1:T(4,128)S(1)}, u32[]{:S(2)}, u32[]{:S(2)}) collective-permute-start(f32[3,1,2048]{2,0,1:T(4,128)S(1)} %copy.500), channel_id=1, source_target_pairs={{0,1},{1,2},{2,3},{3,4},{4,5},{5,6},{6,7},{7,8},{8,9},{9,10},{10,1... | collective-permute-start | bytes 73736 | tf_op jit(solution)/shard_map/ppermute | solution.py:24
  128.8 5.5 %collective-permute-start.12 = (f32[2,1,2048]{2,0,1:T(2,128)S(1)}, f32[2,1,2048]{2,0,1:T(2,128)S(1)}, u32[]{:S(2)}, u32[]{:S(2)}) collective-permute-start(f32[2,1,2048]{2,0,1:T(2,128)S(1)} %get-tuple-element.107), channel_id=1, source_target_pairs={{1,0},{2,1},{3,2},{4,3},{5,4},{6,5},{7,6},{8,7},{9,8},{10,9},{11,1... | collective-permute-start | bytes 49160 | tf_op jit(solution)/shard_map/ppermute | solution.py:26
  130.7 8.4 %collective-permute-start.13 = (f32[2,1,2048]{2,0,1:T(2,128)S(1)}, f32[2,1,2048]{2,0,1:T(2,128)S(1)}, u32[]{:S(2)}, u32[]{:S(2)}) collective-permute-start(f32[2,1,2048]{2,0,1:T(2,128)S(1)} %get-tuple-element.108), channel_id=1, source_target_pairs={{0,1},{1,2},{2,3},{3,4},{4,5},{5,6},{6,7},{7,8},{8,9},{9,10},{10,1... | collective-permute-start | bytes 49160 | tf_op jit(solution)/shard_map/ppermute | solution.py:24
  141.9 9.2 %collective-permute-start.14 = (f32[3,1,2048]{2,0,1:T(4,128)S(1)}, f32[3,1,2048]{2,0,1:T(4,128)S(1)}, u32[]{:S(2)}, u32[]{:S(2)}) collective-permute-start(f32[3,1,2048]{2,0,1:T(4,128)S(1)} %get-tuple-element.53), channel_id=1, source_target_pairs={{0,1},{1,2},{2,3},{3,4},{4,5},{5,6},{6,7},{7,8},{8,9},{9,10},{10,1... | collective-permute-start | bytes 73736 | tf_op jit(solution)/shard_map/ppermute | solution.py:24
  143.9 8.7 %collective-permute-start.15 = (f32[3,1,2048]{2,0,1:T(4,128)S(1)}, f32[3,1,2048]{2,0,1:T(4,128)S(1)}, u32[]{:S(2)}, u32[]{:S(2)}) collective-permute-start(f32[3,1,2048]{2,0,1:T(4,128)S(1)} %get-tuple-element.54), channel_id=1, source_target_pairs={{1,0},{2,1},{3,2},{4,3},{5,4},{6,5},{7,6},{8,7},{9,8},{10,9},{11,1... | collective-permute-start | bytes 73736 | tf_op jit(solution)/shard_map/ppermute | solution.py:26
  155.2 9.1 %collective-permute-start.16 = (f32[2,1,2048]{2,0,1:T(2,128)S(1)}, f32[2,1,2048]{2,0,1:T(2,128)S(1)}, u32[]{:S(2)}, u32[]{:S(2)}) collective-permute-start(f32[2,1,2048]{2,0,1:T(2,128)S(1)} %get-tuple-element.101), channel_id=1, source_target_pairs={{1,0},{2,1},{3,2},{4,3},{5,4},{6,5},{7,6},{8,7},{9,8},{10,9},{11,1... | collective-permute-start | bytes 49160 | tf_op jit(solution)/shard_map/ppermute | solution.py:26
  162.0 8.4 %collective-permute-start.17 = (f32[2,1,2048]{2,0,1:T(2,128)S(1)}, f32[2,1,2048]{2,0,1:T(2,128)S(1)}, u32[]{:S(2)}, u32[]{:S(2)}) collective-permute-start(f32[2,1,2048]{2,0,1:T(2,128)S(1)} %get-tuple-element.102), channel_id=1, source_target_pairs={{0,1},{1,2},{2,3},{3,4},{4,5},{5,6},{6,7},{7,8},{8,9},{9,10},{10,1... | collective-permute-start | bytes 49160 | tf_op jit(solution)/shard_map/ppermute | solution.py:24
  172.9 5.5 %collective-permute-start.19 = (f32[3,1,2048]{2,0,1:T(4,128)S(1)}, f32[3,1,2048]{2,0,1:T(4,128)S(1)}, u32[]{:S(2)}, u32[]{:S(2)}) collective-permute-start(f32[3,1,2048]{2,0,1:T(4,128)S(1)} %copy.503), channel_id=1, source_target_pairs={{1,0},{2,1},{3,2},{4,3},{5,4},{6,5},{7,6},{8,7},{9,8},{10,9},{11,1... | collective-permute-start | bytes 73736 | tf_op jit(solution)/shard_map/ppermute | solution.py:26
  175.2 8.6 %collective-permute-start.18 = (f32[3,1,2048]{2,0,1:T(4,128)S(1)}, f32[3,1,2048]{2,0,1:T(4,128)S(1)}, u32[]{:S(2)}, u32[]{:S(2)}) collective-permute-start(f32[3,1,2048]{2,0,1:T(4,128)S(1)} %copy.502), channel_id=1, source_target_pairs={{0,1},{1,2},{2,3},{3,4},{4,5},{5,6},{6,7},{7,8},{8,9},{9,10},{10,1... | collective-permute-start | bytes 73736 | tf_op jit(solution)/shard_map/ppermute | solution.py:24
  186.2 5.8 %collective-permute-start.20 = (f32[2,1,2048]{2,0,1:T(2,128)S(1)}, f32[2,1,2048]{2,0,1:T(2,128)S(1)}, u32[]{:S(2)}, u32[]{:S(2)}) collective-permute-start(f32[2,1,2048]{2,0,1:T(2,128)S(1)} %get-tuple-element.95), channel_id=1, source_target_pairs={{1,0},{2,1},{3,2},{4,3},{5,4},{6,5},{7,6},{8,7},{9,8},{10,9},{11,1... | collective-permute-start | bytes 49160 | tf_op jit(solution)/shard_map/ppermute | solution.py:26
  188.2 8.4 %collective-permute-start.21 = (f32[2,1,2048]{2,0,1:T(2,128)S(1)}, f32[2,1,2048]{2,0,1:T(2,128)S(1)}, u32[]{:S(2)}, u32[]{:S(2)}) collective-permute-start(f32[2,1,2048]{2,0,1:T(2,128)S(1)} %get-tuple-element.96), channel_id=1, source_target_pairs={{0,1},{1,2},{2,3},{3,4},{4,5},{5,6},{6,7},{7,8},{8,9},{9,10},{10,1... | collective-permute-start | bytes 49160 | tf_op jit(solution)/shard_map/ppermute | solution.py:24
  199.1 5.5 %collective-permute-start.23 = (f32[3,1,2048]{2,0,1:T(4,128)S(1)}, f32[3,1,2048]{2,0,1:T(4,128)S(1)}, u32[]{:S(2)}, u32[]{:S(2)}) collective-permute-start(f32[3,1,2048]{2,0,1:T(4,128)S(1)} %copy.505), channel_id=1, source_target_pairs={{1,0},{2,1},{3,2},{4,3},{5,4},{6,5},{7,6},{8,7},{9,8},{10,9},{11,1... | collective-permute-start | bytes 73736 | tf_op jit(solution)/shard_map/ppermute | solution.py:26
  201.5 8.6 %collective-permute-start.22 = (f32[3,1,2048]{2,0,1:T(4,128)S(1)}, f32[3,1,2048]{2,0,1:T(4,128)S(1)}, u32[]{:S(2)}, u32[]{:S(2)}) collective-permute-start(f32[3,1,2048]{2,0,1:T(4,128)S(1)} %copy.504), channel_id=1, source_target_pairs={{0,1},{1,2},{2,3},{3,4},{4,5},{5,6},{6,7},{7,8},{8,9},{9,10},{10,1... | collective-permute-start | bytes 73736 | tf_op jit(solution)/shard_map/ppermute | solution.py:24
  212.8 5.4 %collective-permute-start.24 = (f32[2,1,2048]{2,0,1:T(2,128)S(1)}, f32[2,1,2048]{2,0,1:T(2,128)S(1)}, u32[]{:S(2)}, u32[]{:S(2)}) collective-permute-start(f32[2,1,2048]{2,0,1:T(2,128)S(1)} %get-tuple-element.87), channel_id=1, source_target_pairs={{1,0},{2,1},{3,2},{4,3},{5,4},{6,5},{7,6},{8,7},{9,8},{10,9},{11,1... | collective-permute-start | bytes 49160 | tf_op jit(solution)/shard_map/ppermute | solution.py:26
  214.7 8.4 %collective-permute-start.25 = (f32[2,1,2048]{2,0,1:T(2,128)S(1)}, f32[2,1,2048]{2,0,1:T(2,128)S(1)}, u32[]{:S(2)}, u32[]{:S(2)}) collective-permute-start(f32[2,1,2048]{2,0,1:T(2,128)S(1)} %get-tuple-element.88), channel_id=1, source_target_pairs={{0,1},{1,2},{2,3},{3,4},{4,5},{5,6},{6,7},{7,8},{8,9},{9,10},{10,1... | collective-permute-start | bytes 49160 | tf_op jit(solution)/shard_map/ppermute | solution.py:24
  225.5 9.2 %collective-permute-start.26 = (f32[3,1,2048]{2,0,1:T(4,128)S(1)}, f32[3,1,2048]{2,0,1:T(4,128)S(1)}, u32[]{:S(2)}, u32[]{:S(2)}) collective-permute-start(f32[3,1,2048]{2,0,1:T(4,128)S(1)} %get-tuple-element.51), channel_id=1, source_target_pairs={{0,1},{1,2},{2,3},{3,4},{4,5},{5,6},{6,7},{7,8},{8,9},{9,10},{10,1... | collective-permute-start | bytes 73736 | tf_op jit(solution)/shard_map/ppermute | solution.py:24
  227.4 8.7 %collective-permute-start.27 = (f32[3,1,2048]{2,0,1:T(4,128)S(1)}, f32[3,1,2048]{2,0,1:T(4,128)S(1)}, u32[]{:S(2)}, u32[]{:S(2)}) collective-permute-start(f32[3,1,2048]{2,0,1:T(4,128)S(1)} %get-tuple-element.52), channel_id=1, source_target_pairs={{1,0},{2,1},{3,2},{4,3},{5,4},{6,5},{7,6},{8,7},{9,8},{10,9},{11,1... | collective-permute-start | bytes 73736 | tf_op jit(solution)/shard_map/ppermute | solution.py:26
  238.7 9.0 %collective-permute-start.28 = (f32[2,1,2048]{2,0,1:T(2,128)S(1)}, f32[2,1,2048]{2,0,1:T(2,128)S(1)}, u32[]{:S(2)}, u32[]{:S(2)}) collective-permute-start(f32[2,1,2048]{2,0,1:T(2,128)S(1)} %get-tuple-element.81), channel_id=1, source_target_pairs={{1,0},{2,1},{3,2},{4,3},{5,4},{6,5},{7,6},{8,7},{9,8},{10,9},{11,1... | collective-permute-start | bytes 49160 | tf_op jit(solution)/shard_map/ppermute | solution.py:26
  245.6 8.4 %collective-permute-start.29 = (f32[2,1,2048]{2,0,1:T(2,128)S(1)}, f32[2,1,2048]{2,0,1:T(2,128)S(1)}, u32[]{:S(2)}, u32[]{:S(2)}) collective-permute-start(f32[2,1,2048]{2,0,1:T(2,128)S(1)} %get-tuple-element.82), channel_id=1, source_target_pairs={{0,1},{1,2},{2,3},{3,4},{4,5},{5,6},{6,7},{7,8},{8,9},{9,10},{10,1... | collective-permute-start | bytes 49160 | tf_op jit(solution)/shard_map/ppermute | solution.py:24
  256.1 5.5 %collective-permute-start.31 = (f32[3,1,2048]{2,0,1:T(4,128)S(1)}, f32[3,1,2048]{2,0,1:T(4,128)S(1)}, u32[]{:S(2)}, u32[]{:S(2)}) collective-permute-start(f32[3,1,2048]{2,0,1:T(4,128)S(1)} %copy.507), channel_id=1, source_target_pairs={{1,0},{2,1},{3,2},{4,3},{5,4},{6,5},{7,6},{8,7},{9,8},{10,9},{11,1... | collective-permute-start | bytes 73736 | tf_op jit(solution)/shard_map/ppermute | solution.py:26
  258.3 8.6 %collective-permute-start.30 = (f32[3,1,2048]{2,0,1:T(4,128)S(1)}, f32[3,1,2048]{2,0,1:T(4,128)S(1)}, u32[]{:S(2)}, u32[]{:S(2)}) collective-permute-start(f32[3,1,2048]{2,0,1:T(4,128)S(1)} %copy.506), channel_id=1, source_target_pairs={{0,1},{1,2},{2,3},{3,4},{4,5},{5,6},{6,7},{7,8},{8,9},{9,10},{10,1... | collective-permute-start | bytes 73736 | tf_op jit(solution)/shard_map/ppermute | solution.py:24
Sparse Core Ops, SparseCore 0:
  11.5 57.1 all-gather.2
  270.1 67.8 all-gather.4
where the time goes:
time: 348 us; the launch traced here: 347 us
  waiting for transfers between devices  129 us (37%)
  starting transfers between devices  127 us (36%)
  local copies, waits for them, and re-layouts  56.8 us (16%)
  between operations  15.6 us (4%)
  other arithmetic  15 us (4%)
    ppermute x16, starting transfers between devices, extended(): lax.ppermute(head, axis, [((i + 1) % count, i) for i in range(count)])  84.2 us
    all_gather x1, waiting for transfers between devices, per_device(): lax.all_gather(drag_blocks[None], 'face', axis=0, tiled=True)  67.3 us
    ppermute x16, waiting for transfers between devices, extended(): lax.ppermute(tail, axis, [(i, (i + 1) % count) for i in range(count)])  50.4 us
    ppermute x16, starting transfers between devices, extended(): lax.ppermute(tail, axis, [(i, (i + 1) % count) for i in range(count)])  42.7 us
    rev x16, local copies, waits for them, and re-layouts, edge_fix(): upper = jnp.where(upper_flip, signs[:, None] * upper[:, ::-1], upper)  22.4 us
    rev x16, local copies, waits for them, and re-layouts, edge_fix(): lower = jnp.where(lower_flip, signs[:, None] * lower[:, ::-1], lower)  22.4 us
    all_gather x1, waiting for transfers between devices, per_device(): lax.all_gather(grouped[None], 'face', axis=0, tiled=True)  11.4 us
  transfers between devices with their start and end apart: 34, of which 15 were waited for; matrix products, arithmetic and copies ran while one was open for 9% of the time, Pallas kernels for 0%

commit v1 on v0

v1 whole, which is shorter than its diff:
```python
import functools

import jax
import jax.numpy as jnp
from jax import lax
from jax.experimental import pallas as pl
from jax.experimental.pallas import tpu as pltpu
from jax.sharding import PartitionSpec as P

MESH = pl.DeviceIdType.MESH
F32 = jnp.float32
BF16 = jnp.bfloat16
ROW = 16
OWN = 8 * ROW


def iota(shape, dim):
    return lax.broadcasted_iota(jnp.int32, shape, dim)


def dot(a, b):
    return jnp.dot(a, b, preferred_element_type=F32)


def flip_lanes(x):
    return jnp.take_along_axis(x, 127 - iota(x.shape, 1), axis=1)


def centred_x(x):
    lane = iota(x.shape, 1)
    ahead = pltpu.roll(x, 127, 1)
    behind = pltpu.roll(x, 1, 1)
    ahead = jnp.where(lane == 127, pltpu.roll(ahead, ROW - 1, 0), ahead)
    behind = jnp.where(lane == 0, pltpu.roll(behind, 1, 0), behind)
    return ahead - behind


def rows_of(ref, first, count):
    return [ref[pl.ds(pl.multiple_of((first + n) * ROW, ROW), ROW), :] for n in range(count)]


def put_row(ref, row, value):
    ref[pl.ds(pl.multiple_of(row * ROW, ROW), ROW), :] = value


def stress_rows(first, count, u_ref, v_ref, stress, p_ref):
    us = rows_of(u_ref, first - 1, count + 2)
    vs = rows_of(v_ref, first - 1, count + 2)
    ps = rows_of(p_ref, first, count)
    old = [rows_of(s, first, count) for s in stress]
    third = F32(2.0 / 3.0)
    for n in range(count):
        e11 = centred_x(us[n + 1])
        e22 = vs[n + 2] - vs[n]
        shear = (us[n + 2] - us[n]) + centred_x(vs[n + 1])
        dd = e11 + e22
        dtn = e11 - e22
        inv = lax.rsqrt(dd * dd + 0.25 * (dtn * dtn + shear * shear) + 0.04)
        grip = ps[n] * inv
        put_row(stress[0], first + n, third * old[0][n] + (grip * dd - ps[n]))
        put_row(stress[1], first + n, third * old[1][n] + 0.25 * (grip * dtn))
        put_row(stress[2], first + n, third * old[2][n] + 0.125 * (grip * shear))


def forcing_row(f_ref, row):
    block = f_ref[pl.ds(pl.multiple_of(row * 64, 64), 64), :].astype(F32)
    return [
        jnp.concatenate([block[8 * c : 8 * c + 8], block[32 + 8 * c : 40 + 8 * c]], axis=0)
        for c in range(4)
    ]


def momentum_rows(first, count, cor, u_ref, v_ref, stress, p_ref, m_ref, f_ref):
    s1 = rows_of(stress[0], first - 1, count + 2)
    s2 = rows_of(stress[1], first - 1, count + 2)
    s12 = rows_of(stress[2], first - 1, count + 2)
    us = rows_of(u_ref, first, count)
    vs = rows_of(v_ref, first, count)
    ps = rows_of(p_ref, first, count)
    ms = rows_of(m_ref, first, count)
    for n in range(count):
        uo, vo, tx, ty = forcing_row(f_ref, first + n)
        u, v, m = us[n], vs[n], ms[n]
        fx = 0.25 * centred_x(s1[n + 1] + s2[n + 1]) + 0.5 * (s12[n + 2] - s12[n])
        fy = 0.5 * centred_x(s12[n + 1]) + 0.25 * ((s1[n + 2] - s2[n + 2]) - (s1[n] - s2[n]))
        du = uo - u
        dv = vo - v
        speed = jnp.sqrt(du * du + dv * dv)
        row = first + n
        turn = jnp.where(row < 8, cor[0], jnp.where(row < 16, cor[1], cor[2])) * m
        inv = jnp.where(ps[n] > 0.0, 1.0 / (m + 0.25 * speed), 0.0)
        put_row(u_ref, first + n, (m * u + 0.25 * (fx + tx + speed * uo + turn * v)) * inv)
        put_row(v_ref, first + n, (m * v + 0.25 * (fy + ty + speed * vo - turn * u)) * inv)


def subcycles(cor, u_ref, v_ref, stress, p_ref, m_ref, f_ref):
    def cycle(k, carry):
        first = 1 + 2 * k

        def stress_part(n, c):
            stress_rows(first + 4 * n, 4, u_ref, v_ref, stress, p_ref)
            return c

        def momentum_part(n, c):
            momentum_rows(
                first + 1 + 4 * n, 4, cor, u_ref, v_ref, stress, p_ref, m_ref, f_ref
            )
            return c

        lax.fori_loop(0, 5 - k, stress_part, 0)
        stress_rows(first + 4 * (5 - k), 2, u_ref, v_ref, stress, p_ref)
        lax.fori_loop(0, 5 - k, momentum_part, 0)
        return carry

    lax.fori_loop(0, 4, cycle, 0)


def kernel(
    forcing_hbm, owner_hbm, mask_hbm, vel_hbm, mass_hbm, strength_hbm,
    vel_out, drag_out,
    x_in, owner_in, mask_in, vel_in, mass_in, strength_in,
    spread, send_f, f_all, u1, v1, p_all, m_all, a1, a2, a12,
    u2, v2, b1, b2, b12, send_d, recv_d, unsort, unsorted, drag_buf, vel_buf,
    in_sem, out_sem, f_send, f_recv, h_send, h_recv, g_send, g_recv, k_send, k_recv, d_send, d_recv,
):
    face = lax.axis_index("face")
    tile = lax.axis_index("tile")
    faces = lax.axis_size("face")
    tiles = lax.axis_size("tile")
    ring = face * tiles + tile
    above = lax.rem(ring + 1, faces * tiles)
    below = lax.rem(ring + faces * tiles - 1, faces * tiles)
    above = (lax.div(above, tiles), lax.rem(above, tiles))
    below = (lax.div(below, tiles), lax.rem(below, tiles))
    others = [(lax.rem(face + d, faces), tile) for d in range(1, faces)]
    odd = lax.rem(lax.div(face, 2), 2)
    swap = 1 - 2 * lax.rem(face, 2)

    barrier = pltpu.get_barrier_semaphore()
    for partner in others + [above, below]:
        pl.semaphore_signal(barrier, inc=1, device_id=partner, device_id_type=MESH)

    loads = [
        pltpu.make_async_copy(src, dst, in_sem.at[n])
        for n, (src, dst) in enumerate(
            [
                (owner_hbm, owner_in),
                (forcing_hbm, x_in),
                (mask_hbm, mask_in),
                (vel_hbm, vel_in),
                (strength_hbm, strength_in),
                (mass_hbm, mass_in),
            ]
        )
    ]
    for load in loads:
        load.start()

    row128 = iota((128, 128), 0)
    lane128 = iota((128, 128), 1)
    eye = row128 == lane128
    ones = jnp.ones((128, 128), BF16)
    mirror = (row128 + lane128 == 127).astype(F32).astype(BF16)
    loads[0].wait()
    owner = owner_in[...]
    owner_lanes = jnp.broadcast_to(owner, (128, 128))
    owner_rows = dot(jnp.where(eye, owner_lanes.astype(F32), 0.0).astype(BF16), ones)
    same = (owner_rows == owner_lanes.astype(F32)) & (row128 <= lane128)
    rank = jnp.sum(same.astype(F32), axis=0, keepdims=True) - 1.0
    owner_odd = (owner & 2) == 2
    rank = jnp.where(owner_odd, 7.0 - rank, rank)
    place = owner.astype(F32) * 8.0 + rank
    place_lanes = jnp.broadcast_to(place, (128, 128))
    sorter = jnp.where(row128.astype(F32) == place_lanes, 1.0, 0.0)
    slot_odd = (row128 & 16) == 16
    sorter = jnp.concatenate(
        [jnp.where(slot_odd, 0.0, sorter), jnp.where(slot_odd, sorter, 0.0)], axis=1
    ).astype(BF16)
    loads[1].wait()
    x = x_in[...]
    spread[0:512, :] = x.astype(F32)
    sign_x = jnp.where((iota((512, 128), 0) & 1) == 0, -1.0, 1.0)
    spread[512:1024, :] = dot(x, mirror) * sign_x
    wide = jnp.concatenate(
        [
            jnp.concatenate(
                [spread[pl.ds(512 * n + c, 128, stride=4), :].astype(BF16) for c in range(4)],
                axis=1,
            )
            for n in range(2)
        ],
        axis=0,
    )
    grouped = dot(sorter, wide)
    for g in range(16):
        send_f[32 * g : 32 * g + 32, :] = jnp.concatenate(
            [grouped[8 * g : 8 * g + 8, 128 * c : 128 * c + 128] for c in range(4)], axis=0
        ).astype(BF16)

    def landing(odd_there):
        return face + odd_there * swap

    pl.semaphore_wait(barrier, faces + 1)

    def forcing_copy(d):
        g = others[d - 1][0]
        there = landing(lax.rem(lax.div(g, 2), 2))
        return pltpu.make_async_remote_copy(
            src_ref=send_f.at[pl.ds(pl.multiple_of(g * 32, 32), 32), :],
            dst_ref=f_all.at[pl.ds(pl.multiple_of(512 + there * 32, 32), 32), :],
            send_sem=f_send.at[d - 1],
            recv_sem=f_recv.at[d - 1],
            device_id=others[d - 1],
            device_id_type=MESH,
        )

    forcing_copies = [forcing_copy(d) for d in range(1, 16)]
    for copy in forcing_copies:
        copy.start()
    f_all[pl.ds(pl.multiple_of(512 + landing(odd) * 32, 32), 32), :] = send_f[
        pl.ds(pl.multiple_of(face * 32, 32), 32), :
    ]

    loads[2].wait()
    mask_lanes = jnp.broadcast_to(mask_in[...].astype(F32), (128, 128))
    flipped = row128 ^ (odd * 15)
    cover = dot(jnp.where(flipped == lane128, mask_lanes, 0.0).astype(BF16), ones)
    for load in loads[3:]:
        load.wait()

    def stage(mirrored):
        for b in range(ROW):
            spot = pl.ds(OWN + (ROW - 1 - b if mirrored else b), 8, stride=ROW)
            cols = slice(128 * b, 128 * b + 128)
            turned = flip_lanes if mirrored else (lambda value: value)
            u = turned(vel_in[0, :, cols])
            u1[spot, :] = -u if mirrored else u
            v1[spot, :] = turned(vel_in[1, :, cols])
            p_all[spot, :] = turned(strength_in[:, cols])
            m_all[spot, :] = turned(mass_in[:, cols])

    @pl.when(odd == 0)
    def _():
        stage(False)

    @pl.when(odd == 1)
    def _():
        stage(True)

    p_all[OWN : OWN + 128, :] = p_all[OWN : OWN + 128, :] * cover * F32(1.0 / 3.0)

    def halo_copies(pairs, send_sem, recv_sem):
        out = []
        for n, (src, dst, up, down) in enumerate(pairs):
            for way, ((lo, hi), there) in enumerate([(up, above), (down, below)]):
                shift = -128 if way == 0 else 128
                out.append(
                    pltpu.make_async_remote_copy(
                        src_ref=src.at[OWN + ROW * lo : OWN + ROW * hi, :],
                        dst_ref=dst.at[OWN + shift + ROW * lo : OWN + shift + ROW * hi, :],
                        send_sem=send_sem.at[2 * n + way],
                        recv_sem=recv_sem.at[2 * n + way],
                        device_id=there,
                        device_id_type=MESH,
                    )
                )
        return out

    first_halo = halo_copies(
        [
            (u1, u1, (0, 8), (0, 8)),
            (v1, v1, (0, 8), (0, 8)),
            (p_all, p_all, (1, 8), (0, 7)),
            (m_all, m_all, (2, 8), (0, 6)),
        ],
        h_send,
        h_recv,
    )
    for copy in first_halo:
        copy.start()

    place_rows = dot(jnp.where(eye, place_lanes, 0.0).astype(BF16), ones)
    unsort[...] = jnp.where(place_rows == lane128.astype(F32), 1.0, 0.0).astype(BF16)
    for ref in (a1, a2, a12):
        ref[...] = jnp.zeros_like(ref)

    for copy in forcing_copies:
        copy.wait_recv()
    forcing_halo = [
        pltpu.make_async_remote_copy(
            src_ref=f_all.at[512 + 64 * lo : 512 + 64 * lo + 384, :],
            dst_ref=f_all.at[512 + shift + 64 * lo : 512 + shift + 64 * lo + 384, :],
            send_sem=g_send.at[way],
            recv_sem=g_recv.at[way],
            device_id=there,
            device_id_type=MESH,
        )
        for way, (lo, shift, there) in enumerate([(2, -512, above), (0, 512, below)])
    ]
    for copy in forcing_halo:
        copy.start()
    for copy in first_halo:
        copy.wait_recv()
    for copy in forcing_halo:
        copy.wait_recv()
    for copy in forcing_copies + first_halo + forcing_halo:
        copy.wait_send()

    cor = [
        0.5 - lax.rem(lax.div(f, 2), 2).astype(F32) for f in (below[0], face, above[0])
    ]
    subcycles(cor, u1, v1, (a1, a2, a12), p_all, m_all, f_all)
    mid_halo = halo_copies(
        [
            (u1, u2, (0, 8), (0, 8)),
            (v1, v2, (0, 8), (0, 8)),
            (a1, b1, (1, 8), (0, 7)),
            (a2, b2, (1, 8), (0, 7)),
            (a12, b12, (1, 8), (0, 7)),
        ],
        k_send,
        k_recv,
    )
    for copy in mid_halo:
        copy.start()
    for src, dst in ((u1, u2), (v1, v2), (a1, b1), (a2, b2), (a12, b12)):
        dst[OWN : OWN + 128, :] = src[OWN : OWN + 128, :]
    for copy in mid_halo:
        copy.wait_recv()
    for copy in mid_halo:
        copy.wait_send()
    subcycles(cor, u2, v2, (b1, b2, b12), p_all, m_all, f_all)

    turn = jnp.where(odd == 1, (row128 + lane128 == 127).astype(F32), eye.astype(F32)).astype(BF16)
    sign_u = (1 - 2 * odd).astype(F32)
    for i in range(8):
        uo, vo, _, _ = forcing_row(f_all, 8 + i)
        (u,), (v,), (p,) = (rows_of(ref, 8 + i, 1) for ref in (u2, v2, p_all))
        du = u - uo
        dv = v - vo
        speed = jnp.where(p > 0.0, jnp.sqrt(du * du + dv * dv), 0.0)
        du = sign_u * (speed * du)
        dv = speed * dv
        both = jnp.concatenate([du[0:8], dv[0:8], du[8:16], dv[8:16]], axis=0).astype(BF16)
        send_d[32 * i : 32 * i + 32, :] = dot(both, turn).astype(BF16)

    def drag_copy(d):
        g = others[d - 1][0]
        from_here = g + odd * (1 - 2 * lax.rem(g, 2))
        return pltpu.make_async_remote_copy(
            src_ref=send_d.at[pl.ds(pl.multiple_of(from_here * 16, 16), 16), :],
            dst_ref=recv_d.at[pl.ds(pl.multiple_of(face * 16, 16), 16), :],
            send_sem=d_send.at[d - 1],
            recv_sem=d_recv.at[d - 1],
            device_id=others[d - 1],
            device_id_type=MESH,
        )

    drag_copies = [drag_copy(d) for d in range(1, 16)]
    for copy in drag_copies:
        copy.start()
    recv_d[pl.ds(pl.multiple_of(face * 16, 16), 16), :] = send_d[
        pl.ds(pl.multiple_of(landing(odd) * 16, 16), 16), :
    ]

    def finish(mirrored):
        for b in range(ROW):
            spot = pl.ds(OWN + (ROW - 1 - b if mirrored else b), 8, stride=ROW)
            cols = slice(128 * b, 128 * b + 128)
            u = u2[spot, :]
            v = v2[spot, :]
            vel_buf[0, :, cols] = -flip_lanes(u) if mirrored else u
            vel_buf[1, :, cols] = flip_lanes(v) if mirrored else v

    @pl.when(odd == 0)
    def _():
        finish(False)

    @pl.when(odd == 1)
    def _():
        finish(True)

    vel_store = pltpu.make_async_copy(vel_buf, vel_out, out_sem.at[0])
    vel_store.start()

    for copy in drag_copies:
        copy.wait_recv()
    back = recv_d[...].astype(F32)
    for c in range(2):
        part = jnp.concatenate(
            [back[16 * g + 8 * c : 16 * g + 8 * c + 8] for g in range(16)], axis=0
        ).astype(BF16)
        unsorted[pl.ds(c, 128, stride=2), :] = dot(unsort[...], part)
    drag_buf[...] = unsorted[...].astype(BF16)
    drag_store = pltpu.make_async_copy(drag_buf, drag_out, out_sem.at[1])
    drag_store.start()
    for copy in drag_copies:
        copy.wait_send()
    vel_store.wait()
    drag_store.wait()


def per_device(ocean_forcing, ice_owner, ice_mask, ice_velocity, ice_mass, ice_strength):
    field = pltpu.VMEM((24 * ROW, 128), F32)
    dma = pltpu.SemaphoreType.DMA
    velocity, drag = pl.pallas_call(
        kernel,
        out_shape=(
            jax.ShapeDtypeStruct((2, 8, 2048), F32),
            jax.ShapeDtypeStruct((256, 128), BF16),
        ),
        in_specs=[pl.BlockSpec(memory_space=pl.ANY)] * 6,
        out_specs=(pl.BlockSpec(memory_space=pl.ANY), pl.BlockSpec(memory_space=pl.ANY)),
        scratch_shapes=[
            pltpu.VMEM((512, 128), BF16),
            pltpu.VMEM((1, 128), jnp.int32),
            pltpu.VMEM((1, 128), jnp.int32),
            pltpu.VMEM((2, 8, 2048), F32),
            pltpu.VMEM((8, 2048), F32),
            pltpu.VMEM((8, 2048), F32),
            pltpu.VMEM((1024, 128), F32),
            pltpu.VMEM((512, 128), BF16),
            pltpu.VMEM((1536, 128), BF16),
        ]
        + [field] * 12
        + [
            pltpu.VMEM((256, 128), BF16),
            pltpu.VMEM((256, 128), BF16),
            pltpu.VMEM((128, 128), BF16),
            pltpu.VMEM((256, 128), F32),
            pltpu.VMEM((256, 128), BF16),
            pltpu.VMEM((2, 8, 2048), F32),
            dma((6,)),
            dma((2,)),
            dma((15,)),
            dma((15,)),
            dma((8,)),
            dma((8,)),
            dma((2,)),
            dma((2,)),
            dma((10,)),
            dma((10,)),
            dma((15,)),
            dma((15,)),
        ],
        compiler_params=pltpu.CompilerParams(
            collective_id=0, has_side_effects=True, vmem_limit_bytes=32 * 2**20
        ),
    )(
        ocean_forcing.reshape(512, 128),
        ice_owner,
        ice_mask,
        ice_velocity.reshape(2, 8, 2048),
        ice_mass.reshape(8, 2048),
        ice_strength.reshape(8, 2048),
    )
    return velocity.reshape(2, 1, 8, 2048), drag.reshape(1, 128, 2, 128)


def solution(mesh):
    in_specs = (
        P("face", "tile", None, None),
        P("face", "tile"),
        P("face", "tile"),
        P(None, "face", "tile", None),
        P("face", "tile", None),
        P("face", "tile", None),
    )
    out_specs = (P(None, "face", "tile", None), P("face", "tile", None, None))
    return jax.shard_map(
        per_device, mesh=mesh, in_specs=in_specs, out_specs=out_specs, check_vma=False
    )
```

time: 348 us -> 64.9 us (0.19)
  waiting for transfers between devices: 129 us -> 0 us
  starting transfers between devices: 127 us -> 0 us
  Pallas kernels: 0 us -> 58.5 us
  local copies, waits for them, and re-layouts: 56.8 us -> 5.43 us
  other arithmetic: 15 us -> 0 us
  between operations: 15.6 us -> 0.66 us
    ppermute x32 -> x0, starting transfers between devices: 127 us -> none  [the longest x16 84.2 us: extended(): lax.ppermute(head, axis, [((i + 1) % count, i) for i in range(count)])]
    all_gather x2 -> x0, waiting for transfers between devices: 78.7 us -> none  [the longest x1 67.3 us: per_device(): lax.all_gather(drag_blocks[None], 'face', axis=0, tiled=True)]
    pallas_call x0 -> x1, Pallas kernels: none -> 58.5 us  [per_device(): pl.pallas_call(kernel, out_shape=(jax.ShapeDtypeStruct((2, 8, 2048), F32)...]
    ppermute x32 -> x0, waiting for transfers between devices: 50.5 us -> none  [the longest x16 50.4 us: extended(): lax.ppermute(tail, axis, [(i, (i + 1) % count) for i in range(count)])]
    rev x32 -> x0, local copies, waits for them, and re-layouts: 44.8 us -> none  [the longest x16 22.4 us: edge_fix(): upper = jnp.where(upper_flip, signs[:, None] * upper[:, ::-1], upper)]
    slice x48 -> x0, local copies, waits for them, and re-layouts: 4.29 us -> none  [the longest x44 3.38 us: slope_x(): return 0.5 * (jnp.roll(inner, -1, -1) - jnp.roll(inner, 1, -1))]
    unnamed x28 -> x14, local copies, waits for them, and re-layouts: 1.5 us -> 5.43 us
    div x29 -> x0, other arithmetic: 3.53 us -> none  [the longest x8 1.07 us: stress_update(): cover * (stress[0] + CE * strength * (dd / delta - 1.0)) / (1.0 + CE)]
  transfers between devices with their start and end apart: 34 -> 0, of which waited for: 15 -> 0; matrix products, arithmetic and copies ran while one was open for 9% -> 0% of each run, Pallas kernels for 0% -> 0%
where the time goes in v1:
time: 64.9 us; the launch traced here: 64.6 us
  Pallas kernels  58.5 us (90%)
  local copies, waits for them, and re-layouts  5.43 us (8%)
  between operations  0.66 us (1%)
    pallas_call x1, Pallas kernels, per_device(): pl.pallas_call(kernel, out_shape=(jax.ShapeDtypeStruct((2, 8, 2048), F32)...  58.5 us
    unnamed x14, local copies, waits for them, and re-layouts  5.43 us

profile of v1, /device:TPU:1, one launch (start us, length us, event | category | flops | bytes accessed | tf_op | source)
XLA Modules:
  0.0 64.6 jit_solution(9068738416370906143)
XLA Ops:
  0.6 0.0 copy-start.4
  0.6 0.0 copy-start.5
  0.7 0.6 copy-done.4
  1.3 0.0 copy-done.5
  1.3 0.0 copy-start
  1.3 0.9 %copy-done = bf16[1,128,4,128]{3,2,1,0:T(4,128)(2,1)S(1)} copy-done((bf16[1,128,4,128]{3,2,1,0:T(4,128)(2,1)S(1)}, bf16[1,128,4,128]{3,2,1,0:T(4,128)(2,1)}, u32[]{:S(2)}) %copy-start) | copy-done | bytes 131096
  2.2 0.0 copy-start.1
  2.2 0.9 %copy-done.1 = f32[2,1,8,2048]{3,2,1,0:T(8,128)S(1)} copy-done((f32[2,1,8,2048]{3,2,1,0:T(8,128)S(1)}, f32[2,1,8,2048]{3,2,1,0:T(8,128)}, u32[]{:S(2)}) %copy-start.1) | copy-done | bytes 131096
  3.1 0.0 copy-start.2
  3.1 0.8 %copy-done.2 = f32[1,8,2048]{2,1,0:T(8,128)S(1)} copy-done((f32[1,8,2048]{2,1,0:T(8,128)S(1)}, f32[1,8,2048]{2,1,0:T(8,128)}, u32[]{:S(2)}) %copy-start.2) | copy-done | bytes 65560
  4.0 0.0 copy-start.3
  4.0 0.8 %copy-done.3 = f32[1,8,2048]{2,1,0:T(8,128)S(1)} copy-done((f32[1,8,2048]{2,1,0:T(8,128)S(1)}, f32[1,8,2048]{2,1,0:T(8,128)}, u32[]{:S(2)}) %copy-start.3) | copy-done | bytes 65560
  4.8 58.5 %shard_map.77 = (f32[2,8,2048]{2,1,0:T(8,128)S(1)}, bf16[256,128]{1,0:T(8,128)(2,1)S(1)}) custom-call(bf16[512,128]{1,0:T(8,128)(2,1)S(1)} %bitcast.8, s32[1,128]{1,0:T(1,128)S(1)} %copy-done.4, s32[1,128]{1,0:T(1,128)S(1)} %copy-done.5, f32[2,8,2048]{2,1,0:T(8,128)S(1)} %bitcast.9, f32[8,2048]{1,0:T(8,128)S(1)} %bitcast.12, f32[8,2048]{1,0:T(8,128)S(1)} %bitcast.13), custom_call_target="tpu_custom_call" | custom-call | tf_op jit(solution)/shard_map/pallas_call | solution.py:406
  63.3 0.7 %copy.11 = f32[2,1,8,2048]{3,2,1,0:T(8,128)} copy(f32[2,1,8,2048]{3,2,1,0:T(8,128)S(1)} %bitcast.10) | data formatting | bytes 262144
  64.0 0.6 copy.12
Async XLA Ops:
  0.6 0.7 %copy-start.4 = (s32[1,128]{1,0:T(1,128)S(1)}, s32[1,128]{1,0:T(1,128)}, u32[]{:S(2)}) copy-start(s32[1,128]{1,0:T(1,128)} %owner_hbm.1) | copy-start | bytes 1540
  0.6 0.7 %copy-start.5 = (s32[1,128]{1,0:T(1,128)S(1)}, s32[1,128]{1,0:T(1,128)}, u32[]{:S(2)}) copy-start(s32[1,128]{1,0:T(1,128)} %mask_hbm.1) | copy-start | bytes 1540
  1.3 0.9 %copy-start = (bf16[1,128,4,128]{3,2,1,0:T(4,128)(2,1)S(1)}, bf16[1,128,4,128]{3,2,1,0:T(4,128)(2,1)}, u32[]{:S(2)}) copy-start(bf16[1,128,4,128]{3,2,1,0:T(4,128)(2,1)} %param.6) | copy-start | bytes 393220
  2.2 0.9 %copy-start.1 = (f32[2,1,8,2048]{3,2,1,0:T(8,128)S(1)}, f32[2,1,8,2048]{3,2,1,0:T(8,128)}, u32[]{:S(2)}) copy-start(f32[2,1,8,2048]{3,2,1,0:T(8,128)} %param.9) | copy-start | bytes 393220
  3.1 0.8 %copy-start.2 = (f32[1,8,2048]{2,1,0:T(8,128)S(1)}, f32[1,8,2048]{2,1,0:T(8,128)}, u32[]{:S(2)}) copy-start(f32[1,8,2048]{2,1,0:T(8,128)} %param.10) | copy-start | bytes 196612
  4.0 0.8 %copy-start.3 = (f32[1,8,2048]{2,1,0:T(8,128)S(1)}, f32[1,8,2048]{2,1,0:T(8,128)}, u32[]{:S(2)}) copy-start(f32[1,8,2048]{2,1,0:T(8,128)} %param.11) | copy-start | bytes 196612

commit v2 on v1

v2 whole, which is shorter than its diff:
```python
import jax
import jax.numpy as jnp
from jax import lax
from jax.experimental import pallas as pl
from jax.experimental.pallas import tpu as pltpu
from jax.sharding import PartitionSpec as P

MESH = pl.DeviceIdType.MESH
F32 = jnp.float32
BF16 = jnp.bfloat16
ROW = 16
OWN = 8 * ROW
F_OWN = 512


def iota(shape, dim):
    return lax.broadcasted_iota(jnp.int32, shape, dim)


def dot(a, b):
    return jnp.dot(a, b, preferred_element_type=F32)


def flip_lanes(x):
    return jnp.take_along_axis(x, 127 - iota(x.shape, 1), axis=1)


def centred_x(x):
    lane = iota(x.shape, 1)
    ahead = pltpu.roll(x, 127, 1)
    behind = pltpu.roll(x, 1, 1)
    ahead = jnp.where(lane == 127, pltpu.roll(ahead, ROW - 1, 0), ahead)
    behind = jnp.where(lane == 0, pltpu.roll(behind, 1, 0), behind)
    return ahead - behind


def rows_of(ref, first, count):
    return [ref[pl.ds(pl.multiple_of((first + n) * ROW, ROW), ROW), :] for n in range(count)]


def put_row(ref, row, value):
    ref[pl.ds(pl.multiple_of(row * ROW, ROW), ROW), :] = value


def stress_rows(first, count, u_ref, v_ref, stress, p_ref):
    us = rows_of(u_ref, first - 1, count + 2)
    vs = rows_of(v_ref, first - 1, count + 2)
    ps = rows_of(p_ref, first, count)
    old = [rows_of(s, first, count) for s in stress]
    third = F32(2.0 / 3.0)
    for n in range(count):
        e11 = centred_x(us[n + 1])
        e22 = vs[n + 2] - vs[n]
        shear = (us[n + 2] - us[n]) + centred_x(vs[n + 1])
        dd = e11 + e22
        dtn = e11 - e22
        inv = lax.rsqrt(dd * dd + 0.25 * (dtn * dtn + shear * shear) + 0.04)
        grip = ps[n] * inv
        put_row(stress[0], first + n, third * old[0][n] + (grip * dd - ps[n]))
        put_row(stress[1], first + n, third * old[1][n] + 0.25 * (grip * dtn))
        put_row(stress[2], first + n, third * old[2][n] + 0.125 * (grip * shear))


def forcing_row(f_ref, row):
    block = f_ref[pl.ds(pl.multiple_of(row * 64, 64), 64), :].astype(F32)
    return [
        jnp.concatenate([block[8 * c : 8 * c + 8], block[32 + 8 * c : 40 + 8 * c]], axis=0)
        for c in range(4)
    ]


def momentum_rows(first, count, cor, u_ref, v_ref, stress, p_ref, m_ref, f_ref):
    s1 = rows_of(stress[0], first - 1, count + 2)
    s2 = rows_of(stress[1], first - 1, count + 2)
    s12 = rows_of(stress[2], first - 1, count + 2)
    us = rows_of(u_ref, first, count)
    vs = rows_of(v_ref, first, count)
    ps = rows_of(p_ref, first, count)
    ms = rows_of(m_ref, first, count)
    for n in range(count):
        uo, vo, tx, ty = forcing_row(f_ref, first + n)
        u, v, m = us[n], vs[n], ms[n]
        fx = 0.25 * centred_x(s1[n + 1] + s2[n + 1]) + 0.5 * (s12[n + 2] - s12[n])
        fy = 0.5 * centred_x(s12[n + 1]) + 0.25 * ((s1[n + 2] - s2[n + 2]) - (s1[n] - s2[n]))
        du = uo - u
        dv = vo - v
        speed = jnp.sqrt(du * du + dv * dv)
        row = first + n
        sign = jnp.where(row < 8, cor[0], jnp.where(row < 16, cor[1], cor[2]))
        turn = sign * m
        inv = jnp.where(ps[n] > 0.0, 1.0 / (m + 0.25 * speed), 0.0)
        put_row(u_ref, first + n, (m * u + 0.25 * (fx + tx + speed * uo + turn * v)) * inv)
        put_row(v_ref, first + n, (m * v + 0.25 * (fy + ty + speed * vo - turn * u)) * inv)


def kernel(
    forcing_hbm, owner_hbm, mask_hbm, vel_hbm, mass_hbm, strength_hbm,
    vel_out, drag_out,
    x_in, owner_in, mask_in, vel_in, mass_in, strength_in,
    spread, send_f, f_all, u_all, v_all, p_all, m_all, a1, a2, a12,
    mid_out, mid_in, send_d, recv_d, unsort, unsorted,
    in_sem, f_send, f_recv, h_send, h_recv, g_send, g_recv,
    k_send, k_recv, d_send, d_recv, edge,
):
    face = lax.axis_index("face")
    tile = lax.axis_index("tile")
    faces = lax.axis_size("face")
    tiles = lax.axis_size("tile")
    ring = face * tiles + tile

    def along(step):
        there = lax.rem(ring + step + faces * tiles, faces * tiles)
        return lax.div(there, tiles), lax.rem(there, tiles)

    above, below = along(1), along(-1)
    chip = lax.div(face, 2)
    odd = lax.rem(chip, 2)
    swap = 1 - 2 * lax.rem(face, 2)
    first = tile == 0
    last = tile == tiles - 1

    def other(n):
        half = lax.div(n + 1, 2)
        return lax.rem(face + 8 + jnp.where(lax.rem(n, 2) == 0, half, -half), faces)

    def remote(src, dst, send_sem, recv_sem, there):
        return pltpu.make_async_remote_copy(
            src_ref=src,
            dst_ref=dst,
            send_sem=send_sem,
            recv_sem=recv_sem,
            device_id=there,
            device_id_type=MESH,
        )

    def rows_at(ref, start, size):
        return ref.at[pl.ds(pl.multiple_of(start, 16), size), :]

    loads = [
        pltpu.make_async_copy(src, dst, in_sem.at[n])
        for n, (src, dst) in enumerate(
            [
                (owner_hbm, owner_in),
                (forcing_hbm, x_in),
                (mask_hbm, mask_in),
                (vel_hbm, vel_in),
                (strength_hbm, strength_in),
                (mass_hbm, mass_in),
            ]
        )
    ]
    for load in loads:
        load.start()

    barrier = pltpu.get_barrier_semaphore()

    def greet(there):
        pl.semaphore_signal(barrier, inc=1, device_id=there, device_id_type=MESH)

    def greet_face(n, carry):
        greet((other(n), tile))
        return carry

    lax.fori_loop(0, 15, greet_face, 0)
    greet(below)

    @pl.when(jnp.logical_not(last))
    def _():
        greet(above)

    row128 = iota((128, 128), 0)
    lane128 = iota((128, 128), 1)
    eye = row128 == lane128
    ones = jnp.ones((128, 128), BF16)
    mirror = (row128 + lane128 == 127).astype(F32).astype(BF16)
    loads[0].wait()
    owner = owner_in[...]
    owner_lanes = jnp.broadcast_to(owner, (128, 128))
    owner_rows = dot(jnp.where(eye, owner_lanes.astype(F32), 0.0).astype(BF16), ones)
    same = (owner_rows == owner_lanes.astype(F32)) & (row128 <= lane128)
    rank = jnp.sum(same.astype(F32), axis=0, keepdims=True) - 1.0
    owner_odd = (owner & 2) == 2
    rank = jnp.where(owner_odd, 7.0 - rank, rank)
    place = owner.astype(F32) * 8.0 + rank
    place_lanes = jnp.broadcast_to(place, (128, 128))
    sorter = jnp.where(row128.astype(F32) == place_lanes, 1.0, 0.0)
    slot_odd = (row128 & 16) == 16
    sorter = jnp.concatenate(
        [jnp.where(slot_odd, 0.0, sorter), jnp.where(slot_odd, sorter, 0.0)], axis=1
    ).astype(BF16)
    loads[1].wait()
    x = x_in[...]
    spread[0:512, :] = x.astype(F32)
    sign_x = jnp.where((iota((512, 128), 0) & 1) == 0, -1.0, 1.0)
    spread[512:1024, :] = dot(x, mirror) * sign_x
    wide = jnp.concatenate(
        [
            jnp.concatenate(
                [spread[pl.ds(512 * n + c, 128, stride=4), :].astype(BF16) for c in range(4)],
                axis=1,
            )
            for n in range(2)
        ],
        axis=0,
    )
    grouped = dot(sorter, wide)
    for g in range(16):
        send_f[32 * g : 32 * g + 32, :] = jnp.concatenate(
            [grouped[8 * g : 8 * g + 8, 128 * c : 128 * c + 128] for c in range(4)], axis=0
        ).astype(BF16)

    def landing(f, odd_there):
        return f + odd_there * (1 - 2 * lax.rem(f, 2))

    pl.semaphore_wait(barrier, faces + jnp.minimum(tile, 1))

    def forcing_copy(n):
        g = other(n)
        there = landing(face, lax.rem(lax.div(g, 2), 2))
        return remote(
            rows_at(send_f, g * 32, 32),
            rows_at(f_all, F_OWN + there * 32, 32),
            f_send.at[n],
            f_recv.at[face],
            (g, tile),
        )

    def forcing_start(n, carry):
        forcing_copy(n).start()
        return carry

    lax.fori_loop(0, 15, forcing_start, 0)

    @pl.when(last)
    def _():
        pl.semaphore_signal(edge, inc=1, device_id=above, device_id_type=MESH)

    f_all[pl.ds(pl.multiple_of(F_OWN + landing(face, odd) * 32, 32), 32), :] = send_f[
        pl.ds(pl.multiple_of(face * 32, 32), 32), :
    ]

    loads[2].wait()
    mask_lanes = jnp.broadcast_to(mask_in[...].astype(F32), (128, 128))
    flipped = row128 ^ (odd * 15)
    cover = dot(jnp.where(flipped == lane128, mask_lanes, 0.0).astype(BF16), ones)
    for load in loads[3:]:
        load.wait()

    def stage(mirrored):
        for b in range(ROW):
            spot = pl.ds(OWN + (ROW - 1 - b if mirrored else b), 8, stride=ROW)
            cols = slice(128 * b, 128 * b + 128)
            turned = flip_lanes if mirrored else (lambda value: value)
            u = turned(vel_in[0, :, cols])
            u_all[spot, :] = -u if mirrored else u
            v_all[spot, :] = turned(vel_in[1, :, cols])
            p_all[spot, :] = turned(strength_in[:, cols])
            m_all[spot, :] = turned(mass_in[:, cols])

    @pl.when(odd == 0)
    def _():
        stage(False)

    @pl.when(odd == 1)
    def _():
        stage(True)

    mine = slice(OWN, OWN + 128)
    p_all[mine, :] = p_all[mine, :] * cover * F32(1.0 / 3.0)

    state = (u_all, v_all, p_all, m_all)

    def state_copies(shift, way, there, send_sem, recv_sem):
        return [
            remote(
                ref.at[OWN : OWN + 128, :],
                ref.at[OWN + shift : OWN + shift + 128, :],
                send_sem.at[2 * n + way],
                recv_sem.at[2 * n + way],
                there,
            )
            for n, ref in enumerate(state)
        ]

    near_up = state_copies(-128, 0, above, h_send, h_recv)
    near_down = state_copies(128, 1, below, h_send, h_recv)

    def start(copies):
        for copy in copies:
            copy.start()

    start(near_up)

    @pl.when(jnp.logical_not(first))
    def _():
        start(near_down)

    place_rows = dot(jnp.where(eye, place_lanes, 0.0).astype(BF16), ones)
    unsort[...] = jnp.where(place_rows == lane128.astype(F32), 1.0, 0.0).astype(BF16)
    for ref in (a1, a2, a12):
        ref[...] = jnp.zeros_like(ref)

    def forcing_row_copy(start, size, way):
        shift = 512 if way else -512
        return remote(
            rows_at(f_all, F_OWN + start, size),
            rows_at(f_all, F_OWN + shift + start, size),
            g_send.at[way],
            g_recv.at[way],
            below if way else above,
        )

    def arrived(f):
        place = landing(f, odd)
        remote(
            rows_at(send_f, 0, 32),
            rows_at(f_all, F_OWN + place * 32, 32),
            f_send.at[0],
            f_recv.at[f],
            above,
        ).wait_recv()

    def pass_row(n, carry):
        step = jnp.where(lax.rem(n, 2) == 1, lax.div(n + 1, 2), 8 - lax.div(n, 2))
        row = lax.rem(chip + step, 8)

        @pl.when(n == 0)
        def _():
            arrived(face + swap)

        @pl.when(n > 0)
        def _():
            arrived(2 * row)
            arrived(2 * row + 1)

        @pl.when(row >= 2)
        def _():
            forcing_row_copy(row * 64, 64, 0).start()

        @pl.when((row < 6) & jnp.logical_not(first))
        def _():
            forcing_row_copy(row * 64, 64, 1).start()

        return carry

    lax.fori_loop(0, 8, pass_row, 0)

    @pl.when(first)
    def _():
        pl.semaphore_wait(edge, 1)
        start(near_down)
        forcing_row_copy(0, 384, 1).start()

    forcing_halo = [forcing_row_copy(128, 384, 0), forcing_row_copy(0, 384, 1)]
    for copy in near_up + near_down + forcing_halo:
        copy.wait_recv()
    for copy in near_up + near_down + forcing_halo:
        copy.wait_send()

    stress = (a1, a2, a12)
    moving = (u_all, v_all, a1, a2, a12)

    def mid_copies(way):
        there = below if way else above
        out = []
        for n in range(5):
            lo, hi = (0, 128) if n < 2 else ((0, 112) if way else (16, 128))
            out.append(
                remote(
                    mid_out.at[n, lo:hi, :],
                    mid_in.at[way, n, lo:hi, :],
                    k_send.at[2 * n + way],
                    k_recv.at[2 * n + way],
                    there,
                )
            )
        return out

    mid_up, mid_down = mid_copies(0), mid_copies(1)

    def middle():
        for n, ref in enumerate(moving):
            mid_out[n] = ref[mine, :]
        start(mid_up + mid_down)
        for copy in mid_up + mid_down:
            copy.wait_recv()
        for n, ref in enumerate(moving):
            lo, hi = (0, 128) if n < 2 else (16, 128)
            ref[OWN - 128 + lo : OWN - 128 + hi, :] = mid_in[0, n, lo:hi, :]
            lo, hi = (0, 128) if n < 2 else (0, 112)
            ref[OWN + 128 + lo : OWN + 128 + hi, :] = mid_in[1, n, lo:hi, :]

    cor = [
        0.5 - lax.rem(lax.div(f, 2), 2).astype(F32)
        for f in (below[0], face, above[0])
    ]

    def cycle(k, carry):
        reach = 7 - 2 * lax.rem(k, 4)
        top = 8 - reach
        bodies = lax.div(reach + 3, 2)

        @pl.when(k == 4)
        def _():
            middle()

        def stress_part(n, c):
            stress_rows(top + 4 * n, 4, u_all, v_all, stress, p_all)
            return c

        def momentum_part(n, c):
            momentum_rows(top + 1 + 4 * n, 4, cor, u_all, v_all, stress, p_all, m_all, f_all)
            return c

        lax.fori_loop(0, bodies, stress_part, 0)
        stress_rows(top + 4 * bodies, 2, u_all, v_all, stress, p_all)
        lax.fori_loop(0, bodies, momentum_part, 0)
        return carry

    lax.fori_loop(0, 8, cycle, 0)

    turn = jnp.where(odd == 1, (row128 + lane128 == 127).astype(F32), eye.astype(F32)).astype(BF16)
    sign_u = (1 - 2 * odd).astype(F32)
    for i in range(8):
        uo, vo, _, _ = forcing_row(f_all, 8 + i)
        (u,), (v,), (p,) = (rows_of(ref, 8 + i, 1) for ref in (u_all, v_all, p_all))
        du = u - uo
        dv = v - vo
        speed = jnp.where(p > 0.0, jnp.sqrt(du * du + dv * dv), 0.0)
        du = sign_u * (speed * du)
        dv = speed * dv
        both = jnp.concatenate([du[0:8], dv[0:8], du[8:16], dv[8:16]], axis=0).astype(BF16)
        send_d[32 * i : 32 * i + 32, :] = dot(both, turn).astype(BF16)

    def drag_copy(n):
        g = other(n)
        return remote(
            rows_at(send_d, landing(g, odd) * 16, 16),
            rows_at(recv_d, face * 16, 16),
            d_send.at[n],
            d_recv.at[n],
            (g, tile),
        )

    def drag_start(n, carry):
        drag_copy(n).start()
        return carry

    lax.fori_loop(0, 15, drag_start, 0)
    recv_d[pl.ds(pl.multiple_of(face * 16, 16), 16), :] = send_d[
        pl.ds(pl.multiple_of(landing(face, odd) * 16, 16), 16), :
    ]

    def finish(mirrored):
        for b in range(ROW):
            spot = pl.ds(OWN + (ROW - 1 - b if mirrored else b), 8, stride=ROW)
            cols = slice(128 * b, 128 * b + 128)
            u = u_all[spot, :]
            v = v_all[spot, :]
            vel_out[0, :, cols] = -flip_lanes(u) if mirrored else u
            vel_out[1, :, cols] = flip_lanes(v) if mirrored else v

    @pl.when(odd == 0)
    def _():
        finish(False)

    @pl.when(odd == 1)
    def _():
        finish(True)

    def sent(n, carry):
        forcing_copy(n).wait_send()
        return carry

    lax.fori_loop(0, 15, sent, 0)

    for copy in mid_up + mid_down:
        copy.wait_send()

    def returned(n, carry):
        drag_copy(n).wait()
        return carry

    lax.fori_loop(0, 15, returned, 0)
    back = recv_d[...].astype(F32)
    for c in range(2):
        part = jnp.concatenate(
            [back[16 * g + 8 * c : 16 * g + 8 * c + 8] for g in range(16)], axis=0
        ).astype(BF16)
        unsorted[pl.ds(c, 128, stride=2), :] = dot(unsort[...], part)
    drag_out[...] = unsorted[...].astype(BF16)


def per_device(ocean_forcing, ice_owner, ice_mask, ice_velocity, ice_mass, ice_strength):
    field = pltpu.VMEM((24 * ROW, 128), F32)
    dma = pltpu.SemaphoreType.DMA
    velocity, drag = pl.pallas_call(
        kernel,
        out_shape=(pltpu.VMEM((2, 8, 2048), F32), pltpu.VMEM((256, 128), BF16)),
        in_specs=[pl.BlockSpec(memory_space=pl.ANY)] * 6,
        out_specs=[pl.BlockSpec(memory_space=pltpu.VMEM)] * 2,
        scratch_shapes=[
            pltpu.VMEM((512, 128), BF16),
            pltpu.VMEM((1, 128), jnp.int32),
            pltpu.VMEM((1, 128), jnp.int32),
            pltpu.VMEM((2, 8, 2048), F32),
            pltpu.VMEM((8, 2048), F32),
            pltpu.VMEM((8, 2048), F32),
            pltpu.VMEM((1024, 128), F32),
            pltpu.VMEM((512, 128), BF16),
            pltpu.VMEM((3 * 512, 128), BF16),
        ]
        + [field] * 7
        + [
            pltpu.VMEM((5, 128, 128), F32),
            pltpu.VMEM((2, 5, 128, 128), F32),
            pltpu.VMEM((256, 128), BF16),
            pltpu.VMEM((256, 128), BF16),
            pltpu.VMEM((128, 128), BF16),
            pltpu.VMEM((256, 128), F32),
            dma((6,)),
            dma((15,)),
            dma((16,)),
            dma((8,)),
            dma((8,)),
            dma((2,)),
            dma((2,)),
            dma((10,)),
            dma((10,)),
            dma((15,)),
            dma((15,)),
            pltpu.SemaphoreType.REGULAR,
        ],
        compiler_params=pltpu.CompilerParams(
            collective_id=0, has_side_effects=True, vmem_limit_bytes=60 * 2**20
        ),
    )(
        ocean_forcing.reshape(512, 128),
        ice_owner,
        ice_mask,
        ice_velocity.reshape(2, 8, 2048),
        ice_mass.reshape(8, 2048),
        ice_strength.reshape(8, 2048),
    )
    return velocity.reshape(2, 1, 8, 2048), drag.reshape(1, 128, 2, 128)


def solution(mesh):
    in_specs = (
        P("face", "tile", None, None),
        P("face", "tile"),
        P("face", "tile"),
        P(None, "face", "tile", None),
        P("face", "tile", None),
        P("face", "tile", None),
    )
    out_specs = (P(None, "face", "tile", None), P("face", "tile", None, None))
    return jax.shard_map(
        per_device, mesh=mesh, in_specs=in_specs, out_specs=out_specs, check_vma=False
    )
```

time: 64.9 us -> 60.9 us (0.938)
  local copies, waits for them, and re-layouts: 5.43 us -> 1.29 us
    unnamed x14 -> x2, local copies, waits for them, and re-layouts: 5.43 us -> 1.29 us
where the time goes in v2:
time: 60.9 us; the launch traced here: 60.8 us
  Pallas kernels  58.8 us (97%)
  local copies, waits for them, and re-layouts  1.29 us (2%)
  between operations  0.64 us (1%)
    pallas_call x1, Pallas kernels, per_device(): pl.pallas_call(kernel, out_shape=(pltpu.VMEM((2, 8, 2048), F32), pltpu.VM...  58.8 us
    unnamed x2, local copies, waits for them, and re-layouts  1.29 us

profile of v2, /device:TPU:1, one launch (start us, length us, event | category | flops | bytes accessed | tf_op | source)
XLA Modules:
  0.0 60.8 jit_solution(15090748231326976508)
XLA Ops:
  0.6 58.8 %shard_map.77 = (f32[2,8,2048]{2,1,0:T(8,128)S(1)}, bf16[256,128]{1,0:T(8,128)(2,1)S(1)}) custom-call(bf16[512,128]{1,0:T(8,128)(2,1)} %bitcast.10, s32[1,128]{1,0:T(1,128)} %owner_hbm.1, s32[1,128]{1,0:T(1,128)} %mask_hbm.1, f32[2,8,2048]{2,1,0:T(8,128)} %bitcast.11, f32[8,2048]{1,0:T(8,128)} %bitcast.12, f32[8,2048]{1,0:T(8,128)} %bitcast.13), custom_call_target="tpu_custom_call" | custom-call | tf_op jit(solution)/shard_map/pallas_call | solution.py:497
  59.5 0.7 %copy.11 = f32[2,1,8,2048]{3,2,1,0:T(8,128)} copy(f32[2,1,8,2048]{3,2,1,0:T(8,128)S(1)} %bitcast.8) | data formatting | bytes 262144
  60.1 0.6 %copy.12 = bf16[1,128,2,128]{3,2,1,0:T(2,128)(2,1)} copy(bf16[1,128,2,128]{3,2,1,0:T(2,128)(2,1)S(1)} %bitcast.9) | data formatting | bytes 131072

commit v3 on v2

--- a/solution.py
+++ b/solution.py
@@ -9,7 +9,7 @@
 F32 = jnp.float32
 BF16 = jnp.bfloat16
 ROW = 16
-OWN = 8 * ROW
+OWN = 9 * ROW
 F_OWN = 512
 
 
@@ -35,11 +35,11 @@
 
 
 def rows_of(ref, first, count):
-    return [ref[pl.ds(pl.multiple_of((first + n) * ROW, ROW), ROW), :] for n in range(count)]
+    return [ref[(first + n) * ROW : (first + n + 1) * ROW, :] for n in range(count)]
 
 
 def put_row(ref, row, value):
-    ref[pl.ds(pl.multiple_of(row * ROW, ROW), ROW), :] = value
+    ref[row * ROW : (row + 1) * ROW, :] = value
 
 
 def stress_rows(first, count, u_ref, v_ref, stress, p_ref):
@@ -62,7 +62,7 @@
 
 
 def forcing_row(f_ref, row):
-    block = f_ref[pl.ds(pl.multiple_of(row * 64, 64), 64), :].astype(F32)
+    block = f_ref[row * 64 : row * 64 + 64, :].astype(F32)
     return [
         jnp.concatenate([block[8 * c : 8 * c + 8], block[32 + 8 * c : 40 + 8 * c]], axis=0)
         for c in range(4)
@@ -78,7 +78,7 @@
     ps = rows_of(p_ref, first, count)
     ms = rows_of(m_ref, first, count)
     for n in range(count):
-        uo, vo, tx, ty = forcing_row(f_ref, first + n)
+        uo, vo, tx, ty = forcing_row(f_ref, first + n - 1)
         u, v, m = us[n], vs[n], ms[n]
         fx = 0.25 * centred_x(s1[n + 1] + s2[n + 1]) + 0.5 * (s12[n + 2] - s12[n])
         fy = 0.5 * centred_x(s12[n + 1]) + 0.25 * ((s1[n + 2] - s2[n + 2]) - (s1[n] - s2[n]))
@@ -86,7 +86,7 @@
         dv = vo - v
         speed = jnp.sqrt(du * du + dv * dv)
         row = first + n
-        sign = jnp.where(row < 8, cor[0], jnp.where(row < 16, cor[1], cor[2]))
+        sign = cor[0] if row < 9 else cor[1] if row < 17 else cor[2]
         turn = sign * m
         inv = jnp.where(ps[n] > 0.0, 1.0 / (m + 0.25 * speed), 0.0)
         put_row(u_ref, first + n, (m * u + 0.25 * (fx + tx + speed * uo + turn * v)) * inv)
@@ -114,10 +114,10 @@
 
     above, below = along(1), along(-1)
     chip = lax.div(face, 2)
+    first = tile == 0
+    last = tile == tiles - 1
     odd = lax.rem(chip, 2)
     swap = 1 - 2 * lax.rem(face, 2)
-    first = tile == 0
-    last = tile == tiles - 1
 
     def other(n):
         half = lax.div(n + 1, 2)
@@ -209,10 +209,73 @@
             [grouped[8 * g : 8 * g + 8, 128 * c : 128 * c + 128] for c in range(4)], axis=0
         ).astype(BF16)
 
+    loads[2].wait()
+    mask_lanes = jnp.broadcast_to(mask_in[...].astype(F32), (128, 128))
+    flipped = row128 ^ (odd * 15)
+    cover = dot(jnp.where(flipped == lane128, mask_lanes, 0.0).astype(BF16), ones)
+    for load in loads[3:]:
+        load.wait()
+
+    def stage(mirrored):
+        for b in range(ROW):
+            spot = pl.ds(OWN + (ROW - 1 - b if mirrored else b), 8, stride=ROW)
+            cols = slice(128 * b, 128 * b + 128)
+            turned = flip_lanes if mirrored else (lambda value: value)
+            u = turned(vel_in[0, :, cols])
+            u_all[spot, :] = -u if mirrored else u
+            v_all[spot, :] = turned(vel_in[1, :, cols])
+            p_all[spot, :] = turned(strength_in[:, cols])
+            m_all[spot, :] = turned(mass_in[:, cols])
+
+    @pl.when(odd == 0)
+    def _():
+        stage(False)
+
+    @pl.when(odd == 1)
+    def _():
+        stage(True)
+
+    mine = slice(OWN, OWN + 128)
+    p_all[mine, :] = p_all[mine, :] * cover * F32(1.0 / 3.0)
+
+    state = (u_all, v_all, p_all, m_all)
+
+    def state_copies(shift, way, there, send_sem, recv_sem):
+        lo = (0, 0, 0, 0) if way else (0, 0, 16, 32)
+        hi = (128, 128, 112, 96) if way else (128, 128, 128, 128)
+        return [
+            remote(
+                ref.at[OWN + lo[n] : OWN + hi[n], :],
+                ref.at[OWN + shift + lo[n] : OWN + shift + hi[n], :],
+                send_sem.at[2 * n + way],
+                recv_sem.at[2 * n + way],
+                there,
+            )
+            for n, ref in enumerate(state)
+        ]
+
+    near_up = state_copies(-128, 0, above, h_send, h_recv)
+    near_down = state_copies(128, 1, below, h_send, h_recv)
+
+    def start(copies):
+        for copy in copies:
+            copy.start()
+
     def landing(f, odd_there):
         return f + odd_there * (1 - 2 * lax.rem(f, 2))
 
-    pl.semaphore_wait(barrier, faces + jnp.minimum(tile, 1))
+    pl.semaphore_wait(barrier, 16 + jnp.minimum(tile, 1))
+
+    @pl.when(last)
+    def _():
+        pl.semaphore_signal(edge, inc=1, device_id=above, device_id_type=MESH)
+
+    start(near_up)
+
+    @pl.when(jnp.logical_not(first))
+    def _():
+        start(near_down)
+
 
     def forcing_copy(n):
         g = other(n)
@@ -231,69 +294,9 @@
 
     lax.fori_loop(0, 15, forcing_start, 0)
 
-    @pl.when(last)
-    def _():
-        pl.semaphore_signal(edge, inc=1, device_id=above, device_id_type=MESH)
-
     f_all[pl.ds(pl.multiple_of(F_OWN + landing(face, odd) * 32, 32), 32), :] = send_f[
         pl.ds(pl.multiple_of(face * 32, 32), 32), :
     ]
-
-    loads[2].wait()
-    mask_lanes = jnp.broadcast_to(mask_in[...].astype(F32), (128, 128))
-    flipped = row128 ^ (odd * 15)
-    cover = dot(jnp.where(flipped == lane128, mask_lanes, 0.0).astype(BF16), ones)
-    for load in loads[3:]:
-        load.wait()
-
-    def stage(mirrored):
-        for b in range(ROW):
-            spot = pl.ds(OWN + (ROW - 1 - b if mirrored else b), 8, stride=ROW)
-            cols = slice(128 * b, 128 * b + 128)
-            turned = flip_lanes if mirrored else (lambda value: value)
-            u = turned(vel_in[0, :, cols])
-            u_all[spot, :] = -u if mirrored else u
-            v_all[spot, :] = turned(vel_in[1, :, cols])
-            p_all[spot, :] = turned(strength_in[:, cols])
-            m_all[spot, :] = turned(mass_in[:, cols])
-
-    @pl.when(odd == 0)
-    def _():
-        stage(False)
-
-    @pl.when(odd == 1)
-    def _():
-        stage(True)
-
-    mine = slice(OWN, OWN + 128)
-    p_all[mine, :] = p_all[mine, :] * cover * F32(1.0 / 3.0)
-
-    state = (u_all, v_all, p_all, m_all)
-
-    def state_copies(shift, way, there, send_sem, recv_sem):
-        return [
-            remote(
-                ref.at[OWN : OWN + 128, :],
-                ref.at[OWN + shift : OWN + shift + 128, :],
-                send_sem.at[2 * n + way],
-                recv_sem.at[2 * n + way],
-                there,
-            )
-            for n, ref in enumerate(state)
-        ]
-
-    near_up = state_copies(-128, 0, above, h_send, h_recv)
-    near_down = state_copies(128, 1, below, h_send, h_recv)
-
-    def start(copies):
-        for copy in copies:
-            copy.start()
-
-    start(near_up)
-
-    @pl.when(jnp.logical_not(first))
-    def _():
-        start(near_down)
 
     place_rows = dot(jnp.where(eye, place_lanes, 0.0).astype(BF16), ones)
     unsort[...] = jnp.where(place_rows == lane128.astype(F32), 1.0, 0.0).astype(BF16)
@@ -351,79 +354,89 @@
         start(near_down)
         forcing_row_copy(0, 384, 1).start()
 
+    cor = [
+        0.5 - lax.rem(lax.div(f, 2), 2).astype(F32) for f in (below[0], face, above[0])
+    ]
+    stress = (a1, a2, a12)
+
+    def stresses(*parts):
+        for lo, hi in parts:
+            stress_rows(9 + lo, hi - lo, u_all, v_all, stress, p_all)
+
+    def velocities(*parts):
+        for lo, hi in parts:
+            momentum_rows(9 + lo, hi - lo, cor, u_all, v_all, stress, p_all, m_all, f_all)
+
+    for copy in near_up + near_down:
+        copy.wait_recv()
+    stresses((-7, 15))
+    for copy in near_up + near_down:
+        copy.wait_send()
+    velocities((0, 8))
+    stresses((1, 7))
+    velocities((2, 6))
+    stresses((3, 5))
     forcing_halo = [forcing_row_copy(128, 384, 0), forcing_row_copy(0, 384, 1)]
-    for copy in near_up + near_down + forcing_halo:
+    for copy in forcing_halo:
         copy.wait_recv()
-    for copy in near_up + near_down + forcing_halo:
-        copy.wait_send()
-
-    stress = (a1, a2, a12)
+    velocities((-6, 0), (8, 14))
+    stresses((-5, 1), (7, 13))
+    velocities((-4, 2), (6, 12))
+    stresses((-3, 3), (5, 11))
+    velocities((-2, 10))
+    stresses((-1, 9))
+    velocities((0, 8))
+
     moving = (u_all, v_all, a1, a2, a12)
 
-    def mid_copies(way):
-        there = below if way else above
-        out = []
-        for n in range(5):
-            lo, hi = (0, 128) if n < 2 else ((0, 112) if way else (16, 128))
-            out.append(
-                remote(
-                    mid_out.at[n, lo:hi, :],
-                    mid_in.at[way, n, lo:hi, :],
-                    k_send.at[2 * n + way],
-                    k_recv.at[2 * n + way],
-                    there,
-                )
-            )
-        return out
-
-    mid_up, mid_down = mid_copies(0), mid_copies(1)
-
-    def middle():
-        for n, ref in enumerate(moving):
-            mid_out[n] = ref[mine, :]
-        start(mid_up + mid_down)
-        for copy in mid_up + mid_down:
-            copy.wait_recv()
-        for n, ref in enumerate(moving):
-            lo, hi = (0, 128) if n < 2 else (16, 128)
-            ref[OWN - 128 + lo : OWN - 128 + hi, :] = mid_in[0, n, lo:hi, :]
-            lo, hi = (0, 128) if n < 2 else (0, 112)
-            ref[OWN + 128 + lo : OWN + 128 + hi, :] = mid_in[1, n, lo:hi, :]
-
-    cor = [
-        0.5 - lax.rem(lax.div(f, 2), 2).astype(F32)
-        for f in (below[0], face, above[0])
-    ]
-
-    def cycle(k, carry):
-        reach = 7 - 2 * lax.rem(k, 4)
-        top = 8 - reach
-        bodies = lax.div(reach + 3, 2)
-
-        @pl.when(k == 4)
-        def _():
-            middle()
-
-        def stress_part(n, c):
-            stress_rows(top + 4 * n, 4, u_all, v_all, stress, p_all)
-            return c
-
-        def momentum_part(n, c):
-            momentum_rows(top + 1 + 4 * n, 4, cor, u_all, v_all, stress, p_all, m_all, f_all)
-            return c
-
-        lax.fori_loop(0, bodies, stress_part, 0)
-        stress_rows(top + 4 * bodies, 2, u_all, v_all, stress, p_all)
-        lax.fori_loop(0, bodies, momentum_part, 0)
-        return carry
-
-    lax.fori_loop(0, 8, cycle, 0)
+    def mid_copy(n, way):
+        lo, hi = [((64, 128), (0, 64), (16, 64)), ((0, 64), (64, 128), (64, 112))][way][n]
+        fields = (slice(0, 5), slice(0, 2), slice(2, 5))[n]
+        return remote(
+            mid_out.at[fields, lo:hi, :],
+            mid_in.at[way, fields, lo:hi, :],
+            k_send.at[2 * n + way],
+            k_recv.at[2 * n + way],
+            below if way else above,
+        )
+
+    mid = [mid_copy(n, way) for n in range(3) for way in range(2)]
+    for n, ref in enumerate(moving):
+        mid_out[n] = ref[mine, :]
+    start(mid)
+
+    def take(n, way, lo, hi):
+        base = OWN + (128 if way else -128)
+        moving[n][base + lo : base + hi, :] = mid_in[way, n, lo:hi, :]
+
+    for copy in mid[:2]:
+        copy.wait_recv()
+    for n in range(5):
+        take(n, 0, 64, 128)
+        take(n, 1, 0, 64)
+    stresses((-3, 11))
+    velocities((-2, 10))
+    stresses((-1, 9))
+    velocities((0, 8))
+    stresses((1, 7))
+    velocities((2, 6))
+    stresses((3, 5))
+    for copy in mid[2:]:
+        copy.wait_recv()
+    for n in range(5):
+        take(n, 0, 0 if n < 2 else 16, 64)
+        take(n, 1, 64, 128 if n < 2 else 112)
+    for lo in (-7, -5, -3, -1):
+        stresses((lo, lo + 4), (4 - lo, 8 - lo))
+        if lo < -1:
+            velocities((lo + 1, lo + 5), (3 - lo, 7 - lo))
+    velocities((0, 8))
 
     turn = jnp.where(odd == 1, (row128 + lane128 == 127).astype(F32), eye.astype(F32)).astype(BF16)
     sign_u = (1 - 2 * odd).astype(F32)
     for i in range(8):
         uo, vo, _, _ = forcing_row(f_all, 8 + i)
-        (u,), (v,), (p,) = (rows_of(ref, 8 + i, 1) for ref in (u_all, v_all, p_all))
+        (u,), (v,), (p,) = (rows_of(ref, 9 + i, 1) for ref in (u_all, v_all, p_all))
         du = u - uo
         dv = v - vo
         speed = jnp.where(p > 0.0, jnp.sqrt(du * du + dv * dv), 0.0)
@@ -474,7 +487,7 @@
 
     lax.fori_loop(0, 15, sent, 0)
 
-    for copy in mid_up + mid_down:
+    for copy in mid + forcing_halo:
         copy.wait_send()
 
     def returned(n, carry):
@@ -492,7 +505,7 @@
 
 
 def per_device(ocean_forcing, ice_owner, ice_mask, ice_velocity, ice_mass, ice_strength):
-    field = pltpu.VMEM((24 * ROW, 128), F32)
+    field = pltpu.VMEM((26 * ROW, 128), F32)
     dma = pltpu.SemaphoreType.DMA
     velocity, drag = pl.pallas_call(
         kernel,
@@ -525,8 +538,8 @@
             dma((8,)),
             dma((2,)),
             dma((2,)),
-            dma((10,)),
-            dma((10,)),
+            dma((6,)),
+            dma((6,)),
             dma((15,)),
             dma((15,)),
             pltpu.SemaphoreType.REGULAR,

time: 60.9 us -> 54.9 us (0.901)
  Pallas kernels: 58.8 us -> 52.9 us
    pallas_call x1, Pallas kernels: 58.8 us -> 52.9 us  [per_device(): pl.pallas_call(kernel, out_shape=(pltpu.VMEM((2, 8, 2048), F32), pltpu.VM...]
where the time goes in v3:
time: 54.9 us; the launch traced here: 54.8 us
  Pallas kernels  52.9 us (96%)
  local copies, waits for them, and re-layouts  1.29 us (2%)
  between operations  0.64 us (1%)
    pallas_call x1, Pallas kernels, per_device(): pl.pallas_call(kernel, out_shape=(pltpu.VMEM((2, 8, 2048), F32), pltpu.VM...  52.9 us
    unnamed x2, local copies, waits for them, and re-layouts  1.29 us

profile of v3, /device:TPU:1, one launch (start us, length us, event | category | flops | bytes accessed | tf_op | source)
XLA Modules:
  0.0 54.8 jit_solution(11624351735134894821)
XLA Ops:
  0.6 52.9 %shard_map.77 = (f32[2,8,2048]{2,1,0:T(8,128)S(1)}, bf16[256,128]{1,0:T(8,128)(2,1)S(1)}) custom-call(bf16[512,128]{1,0:T(8,128)(2,1)} %bitcast.10, s32[1,128]{1,0:T(1,128)} %owner_hbm.1, s32[1,128]{1,0:T(1,128)} %mask_hbm.1, f32[2,8,2048]{2,1,0:T(8,128)} %bitcast.11, f32[8,2048]{1,0:T(8,128)} %bitcast.12, f32[8,2048]{1,0:T(8,128)} %bitcast.13), custom_call_target="tpu_custom_call" | custom-call | tf_op jit(solution)/shard_map/pallas_call | solution.py:510
  53.5 0.7 %copy.11 = f32[2,1,8,2048]{3,2,1,0:T(8,128)} copy(f32[2,1,8,2048]{3,2,1,0:T(8,128)S(1)} %bitcast.8) | data formatting | bytes 262144
  54.1 0.6 %copy.12 = bf16[1,128,2,128]{3,2,1,0:T(2,128)(2,1)} copy(bf16[1,128,2,128]{3,2,1,0:T(2,128)(2,1)S(1)} %bitcast.9) | data formatting | bytes 131072

commit v4 on v3

--- a/solution.py
+++ b/solution.py
@@ -98,7 +98,7 @@
     vel_out, drag_out,
     x_in, owner_in, mask_in, vel_in, mass_in, strength_in,
     spread, send_f, f_all, u_all, v_all, p_all, m_all, a1, a2, a12,
-    mid_out, mid_in, send_d, recv_d, unsort, unsorted,
+    mid_out, mid_in, send_d, recv_d, unsort,
     in_sem, f_send, f_recv, h_send, h_recv, g_send, g_recv,
     k_send, k_recv, d_send, d_recv, edge,
 ):
@@ -140,12 +140,12 @@
         pltpu.make_async_copy(src, dst, in_sem.at[n])
         for n, (src, dst) in enumerate(
             [
-                (owner_hbm, owner_in),
-                (forcing_hbm, x_in),
-                (mask_hbm, mask_in),
                 (vel_hbm, vel_in),
                 (strength_hbm, strength_in),
                 (mass_hbm, mass_in),
+                (mask_hbm, mask_in),
+                (owner_hbm, owner_in),
+                (forcing_hbm, x_in),
             ]
         )
     ]
@@ -161,19 +161,86 @@
         greet((other(n), tile))
         return carry
 
+    greet(below)
+
+    @pl.when(jnp.logical_not(last))
+    def _():
+        greet(above)
+
     lax.fori_loop(0, 15, greet_face, 0)
-    greet(below)
-
-    @pl.when(jnp.logical_not(last))
-    def _():
-        greet(above)
-
     row128 = iota((128, 128), 0)
     lane128 = iota((128, 128), 1)
     eye = row128 == lane128
     ones = jnp.ones((128, 128), BF16)
     mirror = (row128 + lane128 == 127).astype(F32).astype(BF16)
-    loads[0].wait()
+    for load in loads[:4]:
+        load.wait()
+    mask_lanes = jnp.broadcast_to(mask_in[...].astype(F32), (128, 128))
+    flipped = row128 ^ (odd * 15)
+    cover = dot(jnp.where(flipped == lane128, mask_lanes, 0.0).astype(BF16), ones)
+
+    def stage(mirrored):
+        for b in range(ROW):
+            spot = pl.ds(OWN + (ROW - 1 - b if mirrored else b), 8, stride=ROW)
+            cols = slice(128 * b, 128 * b + 128)
+            turned = flip_lanes if mirrored else (lambda value: value)
+            u = turned(vel_in[0, :, cols])
+            u_all[spot, :] = -u if mirrored else u
+            v_all[spot, :] = turned(vel_in[1, :, cols])
+            p_all[spot, :] = turned(strength_in[:, cols])
+            m_all[spot, :] = turned(mass_in[:, cols])
+
+    @pl.when(odd == 0)
+    def _():
+        stage(False)
+
+    @pl.when(odd == 1)
+    def _():
+        stage(True)
+
+    mine = slice(OWN, OWN + 128)
+    p_all[mine, :] = p_all[mine, :] * cover * F32(1.0 / 3.0)
+
+    state = (u_all, v_all, p_all, m_all)
+
+    def state_copies(shift, way, there, send_sem, recv_sem):
+        lo = (0, 0, 0, 0) if way else (0, 0, 16, 32)
+        hi = (128, 128, 112, 96) if way else (128, 128, 128, 128)
+        return [
+            remote(
+                ref.at[OWN + lo[n] : OWN + hi[n], :],
+                ref.at[OWN + shift + lo[n] : OWN + shift + hi[n], :],
+                send_sem.at[2 * n + way],
+                recv_sem.at[2 * n + way],
+                there,
+            )
+            for n, ref in enumerate(state)
+        ]
+
+    near_up = state_copies(-128, 0, above, h_send, h_recv)
+    near_down = state_copies(128, 1, below, h_send, h_recv)
+
+    def start(copies):
+        for copy in copies:
+            copy.start()
+
+    def landing(f, odd_there):
+        return f + odd_there * (1 - 2 * lax.rem(f, 2))
+
+    pl.semaphore_wait(barrier, 16 + jnp.minimum(tile, 1))
+
+    @pl.when(last)
+    def _():
+        pl.semaphore_signal(edge, inc=1, device_id=above, device_id_type=MESH)
+
+    start(near_up)
+
+    @pl.when(jnp.logical_not(first))
+    def _():
+        start(near_down)
+
+
+    loads[4].wait()
     owner = owner_in[...]
     owner_lanes = jnp.broadcast_to(owner, (128, 128))
     owner_rows = dot(jnp.where(eye, owner_lanes.astype(F32), 0.0).astype(BF16), ones)
@@ -188,7 +255,7 @@
     sorter = jnp.concatenate(
         [jnp.where(slot_odd, 0.0, sorter), jnp.where(slot_odd, sorter, 0.0)], axis=1
     ).astype(BF16)
-    loads[1].wait()
+    loads[5].wait()
     x = x_in[...]
     spread[0:512, :] = x.astype(F32)
     sign_x = jnp.where((iota((512, 128), 0) & 1) == 0, -1.0, 1.0)
@@ -209,74 +276,6 @@
             [grouped[8 * g : 8 * g + 8, 128 * c : 128 * c + 128] for c in range(4)], axis=0
         ).astype(BF16)
 
-    loads[2].wait()
-    mask_lanes = jnp.broadcast_to(mask_in[...].astype(F32), (128, 128))
-    flipped = row128 ^ (odd * 15)
-    cover = dot(jnp.where(flipped == lane128, mask_lanes, 0.0).astype(BF16), ones)
-    for load in loads[3:]:
-        load.wait()
-
-    def stage(mirrored):
-        for b in range(ROW):
-            spot = pl.ds(OWN + (ROW - 1 - b if mirrored else b), 8, stride=ROW)
-            cols = slice(128 * b, 128 * b + 128)
-            turned = flip_lanes if mirrored else (lambda value: value)
-            u = turned(vel_in[0, :, cols])
-            u_all[spot, :] = -u if mirrored else u
-            v_all[spot, :] = turned(vel_in[1, :, cols])
-            p_all[spot, :] = turned(strength_in[:, cols])
-            m_all[spot, :] = turned(mass_in[:, cols])
-
-    @pl.when(odd == 0)
-    def _():
-        stage(False)
-
-    @pl.when(odd == 1)
-    def _():
-        stage(True)
-
-    mine = slice(OWN, OWN + 128)
-    p_all[mine, :] = p_all[mine, :] * cover * F32(1.0 / 3.0)
-
-    state = (u_all, v_all, p_all, m_all)
-
-    def state_copies(shift, way, there, send_sem, recv_sem):
-        lo = (0, 0, 0, 0) if way else (0, 0, 16, 32)
-        hi = (128, 128, 112, 96) if way else (128, 128, 128, 128)
-        return [
-            remote(
-                ref.at[OWN + lo[n] : OWN + hi[n], :],
-                ref.at[OWN + shift + lo[n] : OWN + shift + hi[n], :],
-                send_sem.at[2 * n + way],
-                recv_sem.at[2 * n + way],
-                there,
-            )
-            for n, ref in enumerate(state)
-        ]
-
-    near_up = state_copies(-128, 0, above, h_send, h_recv)
-    near_down = state_copies(128, 1, below, h_send, h_recv)
-
-    def start(copies):
-        for copy in copies:
-            copy.start()
-
-    def landing(f, odd_there):
-        return f + odd_there * (1 - 2 * lax.rem(f, 2))
-
-    pl.semaphore_wait(barrier, 16 + jnp.minimum(tile, 1))
-
-    @pl.when(last)
-    def _():
-        pl.semaphore_signal(edge, inc=1, device_id=above, device_id_type=MESH)
-
-    start(near_up)
-
-    @pl.when(jnp.logical_not(first))
-    def _():
-        start(near_down)
-
-
     def forcing_copy(n):
         g = other(n)
         there = landing(face, lax.rem(lax.div(g, 2), 2))
@@ -298,8 +297,14 @@
         pl.ds(pl.multiple_of(face * 32, 32), 32), :
     ]
 
-    place_rows = dot(jnp.where(eye, place_lanes, 0.0).astype(BF16), ones)
-    unsort[...] = jnp.where(place_rows == lane128.astype(F32), 1.0, 0.0).astype(BF16)
+    row256 = iota((256, 128), 0)
+    lane256 = iota((256, 128), 1)
+    picked = jnp.where(row256 // 2 == lane256, jnp.broadcast_to(place, (256, 128)), 0.0)
+    place_rows = dot(picked.astype(BF16), ones)
+    slot = (lane256 // 16) * 8 + lane256 % 8
+    slot = jnp.where(row256 % 2 == lane256 // 8 % 2, slot, -128).astype(F32)
+    unsort[:, 0:128] = jnp.where(place_rows == slot, 1.0, 0.0).astype(BF16)
+    unsort[:, 128:256] = jnp.where(place_rows - 64.0 == slot, 1.0, 0.0).astype(BF16)
     for ref in (a1, a2, a12):
         ref[...] = jnp.zeros_like(ref)
 
@@ -455,11 +460,8 @@
             (g, tile),
         )
 
-    def drag_start(n, carry):
-        drag_copy(n).start()
-        return carry
-
-    lax.fori_loop(0, 15, drag_start, 0)
+    drag_copies = [drag_copy(n) for n in range(15)]
+    start(drag_copies)
     recv_d[pl.ds(pl.multiple_of(face * 16, 16), 16), :] = send_d[
         pl.ds(pl.multiple_of(landing(face, odd) * 16, 16), 16), :
     ]
@@ -490,18 +492,11 @@
     for copy in mid + forcing_halo:
         copy.wait_send()
 
-    def returned(n, carry):
-        drag_copy(n).wait()
-        return carry
-
-    lax.fori_loop(0, 15, returned, 0)
-    back = recv_d[...].astype(F32)
-    for c in range(2):
-        part = jnp.concatenate(
-            [back[16 * g + 8 * c : 16 * g + 8 * c + 8] for g in range(16)], axis=0
-        ).astype(BF16)
-        unsorted[pl.ds(c, 128, stride=2), :] = dot(unsort[...], part)
-    drag_out[...] = unsorted[...].astype(BF16)
+    for copy in drag_copies:
+        copy.wait_recv()
+    drag_out[...] = dot(unsort[...], recv_d[...]).astype(BF16)
+    for copy in drag_copies:
+        copy.wait_send()
 
 
 def per_device(ocean_forcing, ice_owner, ice_mask, ice_velocity, ice_mass, ice_strength):
@@ -529,8 +524,7 @@
             pltpu.VMEM((2, 5, 128, 128), F32),
             pltpu.VMEM((256, 128), BF16),
             pltpu.VMEM((256, 128), BF16),
-            pltpu.VMEM((128, 128), BF16),
-            pltpu.VMEM((256, 128), F32),
+            pltpu.VMEM((256, 256), BF16),
             dma((6,)),
             dma((15,)),
             dma((16,)),

time: 54.9 us -> 54.9 us (level)
  no operation moved by 1% of the time
where the time goes in v4:
time: 54.9 us; the launch traced here: 54.8 us
  Pallas kernels  52.9 us (96%)
  local copies, waits for them, and re-layouts  1.29 us (2%)
  between operations  0.64 us (1%)
    pallas_call x1, Pallas kernels, per_device(): pl.pallas_call(kernel, out_shape=(pltpu.VMEM((2, 8, 2048), F32), pltpu.VM...  52.9 us
    unnamed x2, local copies, waits for them, and re-layouts  1.29 us

profile of v4, /device:TPU:1, one launch (start us, length us, event | category | flops | bytes accessed | tf_op | source)
XLA Modules:
  0.0 54.8 jit_solution(6075504634366407698)
XLA Ops:
  0.6 52.9 %shard_map.77 = (f32[2,8,2048]{2,1,0:T(8,128)S(1)}, bf16[256,128]{1,0:T(8,128)(2,1)S(1)}) custom-call(bf16[512,128]{1,0:T(8,128)(2,1)} %bitcast.10, s32[1,128]{1,0:T(1,128)} %owner_hbm.1, s32[1,128]{1,0:T(1,128)} %mask_hbm.1, f32[2,8,2048]{2,1,0:T(8,128)} %bitcast.11, f32[8,2048]{1,0:T(8,128)} %bitcast.12, f32[8,2048]{1,0:T(8,128)} %bitcast.13), custom_call_target="tpu_custom_call" | custom-call | tf_op jit(solution)/shard_map/pallas_call | solution.py:505
  53.5 0.7 %copy.11 = f32[2,1,8,2048]{3,2,1,0:T(8,128)} copy(f32[2,1,8,2048]{3,2,1,0:T(8,128)S(1)} %bitcast.8) | data formatting | bytes 262144
  54.2 0.6 %copy.12 = bf16[1,128,2,128]{3,2,1,0:T(2,128)(2,1)} copy(bf16[1,128,2,128]{3,2,1,0:T(2,128)(2,1)S(1)} %bitcast.9) | data formatting | bytes 131072

commit v5 on v3

--- a/solution.py
+++ b/solution.py
@@ -385,13 +385,15 @@
     stresses((-3, 3), (5, 11))
     velocities((-2, 10))
     stresses((-1, 9))
-    velocities((0, 8))
 
     moving = (u_all, v_all, a1, a2, a12)
 
     def mid_copy(n, way):
-        lo, hi = [((64, 128), (0, 64), (16, 64)), ((0, 64), (64, 128), (64, 112))][way][n]
-        fields = (slice(0, 5), slice(0, 2), slice(2, 5))[n]
+        lo, hi = [
+            ((64, 128), (64, 128), (16, 64), (0, 64)),
+            ((0, 64), (0, 64), (64, 112), (64, 128)),
+        ][way][n]
+        fields = slice(0, 2) if n % 2 else slice(2, 5)
         return remote(
             mid_out.at[fields, lo:hi, :],
             mid_in.at[way, fields, lo:hi, :],
@@ -400,16 +402,20 @@
             below if way else above,
         )
 
-    mid = [mid_copy(n, way) for n in range(3) for way in range(2)]
-    for n, ref in enumerate(moving):
-        mid_out[n] = ref[mine, :]
-    start(mid)
+    mid = [mid_copy(n, way) for n in range(4) for way in range(2)]
+    for n in range(2, 5):
+        mid_out[n] = moving[n][mine, :]
+    start(mid[:2])
+    velocities((0, 8))
+    for n in range(2):
+        mid_out[n] = moving[n][mine, :]
+    start(mid[2:])
 
     def take(n, way, lo, hi):
         base = OWN + (128 if way else -128)
         moving[n][base + lo : base + hi, :] = mid_in[way, n, lo:hi, :]
 
-    for copy in mid[:2]:
+    for copy in mid[:4]:
         copy.wait_recv()
     for n in range(5):
         take(n, 0, 64, 128)
@@ -421,7 +427,7 @@
     stresses((1, 7))
     velocities((2, 6))
     stresses((3, 5))
-    for copy in mid[2:]:
+    for copy in mid[4:]:
         copy.wait_recv()
     for n in range(5):
         take(n, 0, 0 if n < 2 else 16, 64)
@@ -538,8 +544,8 @@
             dma((8,)),
             dma((2,)),
             dma((2,)),
-            dma((6,)),
-            dma((6,)),
+            dma((8,)),
+            dma((8,)),
             dma((15,)),
             dma((15,)),
             pltpu.SemaphoreType.REGULAR,

time: 54.9 us -> 54.8 us (level)
  no operation moved by 1% of the time
where the time goes in v5:
time: 54.8 us; the launch traced here: 54.7 us
  Pallas kernels  52.8 us (96%)
  local copies, waits for them, and re-layouts  1.29 us (2%)
  between operations  0.64 us (1%)
    pallas_call x1, Pallas kernels, per_device(): pl.pallas_call(kernel, out_shape=(pltpu.VMEM((2, 8, 2048), F32), pltpu.VM...  52.8 us
    unnamed x2, local copies, waits for them, and re-layouts  1.29 us

profile of v5, /device:TPU:1, one launch (start us, length us, event | category | flops | bytes accessed | tf_op | source)
XLA Modules:
  0.0 54.7 jit_solution(17552749455687002362)
XLA Ops:
  0.6 52.8 %shard_map.77 = (f32[2,8,2048]{2,1,0:T(8,128)S(1)}, bf16[256,128]{1,0:T(8,128)(2,1)S(1)}) custom-call(bf16[512,128]{1,0:T(8,128)(2,1)} %bitcast.10, s32[1,128]{1,0:T(1,128)} %owner_hbm.1, s32[1,128]{1,0:T(1,128)} %mask_hbm.1, f32[2,8,2048]{2,1,0:T(8,128)} %bitcast.11, f32[8,2048]{1,0:T(8,128)} %bitcast.12, f32[8,2048]{1,0:T(8,128)} %bitcast.13), custom_call_target="tpu_custom_call" | custom-call | tf_op jit(solution)/shard_map/pallas_call | solution.py:516
  53.4 0.7 %copy.11 = f32[2,1,8,2048]{3,2,1,0:T(8,128)} copy(f32[2,1,8,2048]{3,2,1,0:T(8,128)S(1)} %bitcast.8) | data formatting | bytes 262144
  54.0 0.6 %copy.12 = bf16[1,128,2,128]{3,2,1,0:T(2,128)(2,1)} copy(bf16[1,128,2,128]{3,2,1,0:T(2,128)(2,1)S(1)} %bitcast.9) | data formatting | bytes 131072
